TPU v7x, 128 devices: a whole 4x4x4 slice. The times are simulated.
128 devices in a mesh: dom: 32 (over z, y, core), rep: 4 (over x).
Axes of the slice: x: 4, y: 4, z: 4, core: 2. Of those that a mesh axis runs over, the one named last changes fastest.
Arguments:
- own_values: bfloat16 [32768, 1024], P('dom'), may hold values from -6 to 6
- own_scale: bfloat16 [256], P('dom'), may hold values from 0.25 to 4
- halo_cache: bfloat16 [131072, 1024], P('dom'), may hold values from -6 to 6
- send_list: int32 [32, 32], P('dom'), may hold values from 0 to 7
- batch_ids: int32 [32, 64], P('dom', 'rep'), may hold values from 0 to 7
- neighbor_blocks: int32 [32, 64, 6], P('dom', 'rep'), may hold values from 0 to 39, as said below
- edge_tiles: bfloat16 [32, 64, 6, 128, 128], P('dom', 'rep'), may hold values from -0.21875 to 0.21875
- w_self: bfloat16 [1024, 1024], replicated, may hold values from -0.1875 to 0.1875
- w_neigh: bfloat16 [1024, 1024], replicated, may hold values from -0.1875 to 0.1875
- cotangent: bfloat16 [262144, 1024], P(('dom', 'rep')), may hold values from -6 to 6
Outputs:
- output_rows: bfloat16 [262144, 1024], P(('dom', 'rep'))
- grad_weights: float32 [2048, 1024], P(('dom', 'rep'))
Inputs may be any that keep to these rules, and one draw needn't show every extreme that they name: `neighbor_blocks`: entries below 8 name a partition's own blocks, 8 + p names the block received from partition p; the rows of each device name every one of the 32 received blocks, and block 0 at least once.
All inputs are finite; a program needn't handle non-finite values.
Results may differ from a plain program's by a relative error of at most 0.014.
Values may be sent and summed in bfloat16 or wider, within the bound.
A program may use at most 192 MiB of HBM per device.

v0:
```python
import math

import jax
import jax.numpy as jnp
from jax import lax
from jax.sharding import PartitionSpec as P

MOMENTUM = 0.6


def on_device(
    own_values,
    own_scale,
    halo_cache,
    send_list,
    batch_ids,
    neighbor_blocks,
    edge_tiles,
    w_self,
    w_neigh,
    cotangent,
):
    feat_width = own_values.shape[1]
    block_rows = edge_tiles.shape[-1]
    part_count = lax.axis_size("dom")
    rep_count = lax.axis_size("rep")
    own_blocks = own_values.reshape(-1, block_rows, feat_width)
    chosen = send_list[0]
    outgoing = jnp.take(own_blocks, chosen, axis=0)
    out_scale = jnp.take(own_scale, chosen, axis=0)
    caches = halo_cache.reshape(-1, block_rows, feat_width)
    fresh_vals, fresh_scale = (
        lax.all_to_all(outgoing, "dom", split_axis=0, concat_axis=0, tiled=True),
        lax.all_to_all(out_scale, "dom", split_axis=0, concat_axis=0, tiled=True),
    )
    fresh_rows = fresh_vals.astype(jnp.float32) * fresh_scale.astype(jnp.float32)[:, None, None]
    halo_rows = (MOMENTUM * fresh_rows + (1.0 - MOMENTUM) * caches.astype(jnp.float32)).astype(
        jnp.bfloat16
    )
    scales = own_scale.astype(jnp.float32)
    own_deq = (own_blocks.astype(jnp.float32) * scales[:, None, None]).astype(jnp.bfloat16)
    lookup = jnp.concatenate([own_deq, halo_rows], axis=0)
    gathered = jnp.take(lookup, neighbor_blocks[0], axis=0)
    summed = jnp.einsum(
        "tkij,tkjd->tid", edge_tiles[0], gathered, preferred_element_type=jnp.float32
    ).astype(jnp.bfloat16)
    self_flat = jnp.take(own_deq, batch_ids[0], axis=0).reshape(-1, feat_width)
    summed_flat = summed.reshape(-1, feat_width)
    pre_act = jnp.dot(self_flat, w_self, preferred_element_type=jnp.float32) + jnp.dot(
        summed_flat, w_neigh, preferred_element_type=jnp.float32
    )
    sigmoid_z = jax.nn.sigmoid(pre_act)
    output_rows = (pre_act * sigmoid_z).astype(jnp.bfloat16)
    delta = (
        cotangent.astype(jnp.float32) * sigmoid_z * (1.0 + pre_act * (1.0 - sigmoid_z))
    ).astype(jnp.bfloat16)
    stacked = jnp.concatenate([self_flat, summed_flat], axis=1)
    grad_share = lax.psum_scatter(
        lax.dot_general(
            stacked, delta, (((0,), (0,)), ((), ())), preferred_element_type=jnp.float32
        ),
        ("dom", "rep"),
        scatter_dimension=0,
        tiled=True,
    )
    total_rows = stacked.shape[0] * part_count * rep_count
    return (output_rows, grad_share * (1.0 / math.sqrt(total_rows)))


def solution(mesh):
    placed = (
        P("dom", None),
        P("dom"),
        P("dom", None),
        P("dom", None),
        P("dom", "rep"),
        P("dom", "rep", None),
        P("dom", "rep", None, None, None),
        P(),
        P(),
        P(("dom", "rep"), None),
    )
    return jax.shard_map(
        on_device,
        mesh=mesh,
        in_specs=placed,
        out_specs=(P(("dom", "rep"), None), P(("dom", "rep"), None)),
        check_vma=False,
    )
```

profile of v0, /device:TPU:0, one launch (start us, length us, event | category | flops | bytes accessed | tf_op | source)
XLA Modules:
  0.0 881.0 jit_solution(15762938132335885253)
XLA Ops:
  7.2 0.0 copy-start
  7.2 0.8 fusion.13
  8.0 1.5 gather_fusion.2
  9.5 0.7 and_select_fusion
  10.2 0.7 copy.20
  10.9 8.4 all-to-all-start.1
  19.3 0.7 compare_and_fusion.1
  20.0 6.5 gather_fusion.1
  26.5 7.5 broadcast_select_fusion
  34.0 0.0 copy-start.2
  34.0 0.0 copy-start.6
  34.0 0.0 copy-start.9
  34.0 0.0 all-to-all-done.1
  34.0 7.7 all-to-all-start
  41.7 0.2 reduce-scatter.2.cloned.1.call-start
  41.9 0.0 copy-done.2
  41.9 0.0 copy-done.6
  41.9 0.1 copy.21
  42.0 0.1 reshape.195
  42.1 0.1 copy.19
  42.2 0.0 copy-done.9
  42.2 3.8 multiply_convert_fusion.3
  46.0 4.4 gather_fusion
  50.4 0.0 copy-start.8
  50.5 0.1 broadcast_bitcast_fusion
  50.5 2.6 bitcast_select_fusion
  53.2 0.0 copy-start.4
  53.2 2.1 copy-done.4
  55.3 0.0 copy-done.8
  55.3 6.7 fusion.17
  61.9 11.5 %convert_multiply_fusion = f32[4096,1024]{1,0:T(8,128)} fusion(bf16[4096,1024]{1,0:T(8,128)(2,1)} %param.12), kind=kLoop, calls=%fused_computation.8 | loop fusion | flops 8388608 | bytes 25165824 | tf_op jit(solution)/shard_map/mul | solution.py:37
  73.5 0.3 convert_reduce_fusion
  73.8 73.7 %all-to-all-done = bf16[32,128,1024]{2,1,0:T(8,128)(2,1)} async-done(((bf16[32,128,1024]{2,1,0:T(8,128)(2,1)}), bf16[32,128,1024]{2,1,0:T(8,128)(2,1)}, u32[]{:S(2)}, u32[]{:S(2)}) %all-to-all-start) | async-done | bytes 8388640 | tf_op jit(solution)/shard_map/all_to_all | solution.py:33
  147.5 0.0 copy-start.3
  147.5 9.5 %add_convert_fusion = bf16[32,128,1024]{2,1,0:T(8,128)(2,1)S(1)} fusion(f32[32,128,1024]{2,1,0:T(8,128)} %bitcast.44, bf16[32,128,1024]{2,1,0:T(8,128)(2,1)} %all-to-all-done, f32[32]{0:T(128)S(1)} %convert_reduce_fusion), kind=kLoop, calls=%fused_computation.7 | loop fusion | flops 20971520 | bytes 33554560 | tf_op jit(solution)/shard_map/convert_element_type | solution.py:37
  157.1 0.0 copy-done.3
  157.1 6.3 pad_maximum_fusion
  163.4 14.2 %gather_fusion.3 = bf16[96,128,1024]{2,1,0:T(8,128)(2,1)} fusion(bf16[40,128,1024]{2,1,0:T(8,128)(2,1)} %pad_maximum_fusion, s32[1024]{0:T(1024)S(1)} %pad_clamp_fusion), kind=kCustom, calls=%fused_computation.3 | custom fusion | bytes 50332032 | tf_op jit(solution)/shard_map/jit(_take)/gather | solution.py:43
  177.5 0.0 copy-done
  177.6 12.1 %bitcast_convert_fusion = bf16[16,1024,128]{1,2,0:T(8,128)(2,1)} fusion(bf16[16,6,128,1024]{3,2,1,0:T(8,128)(2,1)} %bitcast.47, pred[16,6]{1,0:T(8,128)(4,1)S(1)} %copy.19, bf16[1,16,6,128,128]{4,3,2,1,0:T(8,128)(2,1)S(1)} %copy-done), kind=kOutput, calls=%fused_computation.15 | convolution fusion | flops 3235905536 | bytes 32505952 | tf_op jit(solution)/shard_map/tkij,tkjd->tid/dot_general | solution.py:44
  189.6 15.7 %multiply_convert_fusion.1 = (bf16[2048,1024]{1,0:T(8,128)(2,1)}, f32[2048,1024]{1,0:T(8,128)}) fusion(f32[2048,1024]{1,0:T(8,128)} %fusion.17, bf16[2048,1024]{1,0:T(8,128)(2,1)} %bitcast.48, bf16[1024,1024]{1,0:T(8,128)(2,1)} %param.18), kind=kOutput, calls=%fused_computation.17 | convolution fusion | flops 4307550208 | bytes 27262976 | tf_op jit(solution)/shard_map/dot_general | solution.py:49
  205.3 0.0 copy-done.5
  205.3 0.0 copy-done.7
  205.3 17.4 %fusion.4 = f32[2048,1024]{1,0:T(8,128)} fusion(bf16[2048,1024]{1,0:T(8,128)(2,1)} %bitcast.49, bf16[2048,1024]{1,0:T(8,128)(2,1)S(1)} %copy-done.5, f32[2048,1024]{1,0:T(8,128)} %get-tuple-element.3, bf16[2048,1024]{1,0:T(8,128)(2,1)S(1)} %copy-done.7), kind=kOutput, calls=%fused_computation.11 | convolution fusion | flops 8627683328 | bytes 29360128 | tf_op jit(solution)/shard_map/dot_general | solution.py:59
  222.7 0.0 reduce-scatter.2.cloned.1.call-update
  222.8 649.9 %reduce-scatter.2.cloned.1.call-done = f32[16,1024]{1,0:T(8,128)} async-done(((f32[2048,1024]{1,0:T(8,128)}), f32[16,1024]{1,0:T(8,128)}) %reduce-scatter.2.cloned.1.call-update) | async-done | bytes 65552 | tf_op jit(solution)/shard_map/reduce_scatter | solution.py:58
  872.7 1.5 broadcast_multiply_fusion
  874.1 0.0 copy-done.1
  (11 shorter events, 0.1 us)
Async XLA Ops:
  7.2 170.4 %copy-start = (bf16[1,16,6,128,128]{4,3,2,1,0:T(8,128)(2,1)S(1)}, bf16[1,16,6,128,128]{4,3,2,1,0:T(8,128)(2,1)}, u32[]{:S(2)}) copy-start(bf16[1,16,6,128,128]{4,3,2,1,0:T(8,128)(2,1)} %param.16) | copy-start | bytes 9437188
  10.9 23.1 %all-to-all-start.1 = ((bf16[32,1,1]{2,1,0:T(2,128)(2,1)}), bf16[32,1,1]{2,1,0:T(2,128)(2,1)S(1)}, u32[]{:S(2)}, u32[]{:S(2)}) async-start(bf16[32,1,1]{2,1,0:T(2,128)(2,1)} %copy.20), calls=%async_computation.1 | async-start | bytes 32768 | tf_op jit(solution)/shard_map/all_to_all | solution.py:34
  34.0 7.9 copy-start.2
  34.0 7.9 copy-start.6
  34.0 8.3 copy-start.9
  34.0 113.6 %all-to-all-start = ((bf16[32,128,1024]{2,1,0:T(8,128)(2,1)}), bf16[32,128,1024]{2,1,0:T(8,128)(2,1)}, u32[]{:S(2)}, u32[]{:S(2)}) async-start(bf16[32,128,1024]{2,1,0:T(8,128)(2,1)} %broadcast_select_fusion), calls=%async_computation | async-start | bytes 16777216 | tf_op jit(solution)/shard_map/all_to_all | solution.py:33
  41.7 831.0 %reduce-scatter.2.cloned.1.call-start = ((), (), s32[]{:S(2)}) async-start(), calls=%async_computation.3 | async-start | bytes 8454144 | tf_op jit(solution)/shard_map/reduce_scatter | solution.py:58
  50.4 4.8 copy-start.8
  53.2 2.1 copy-start.4
  147.5 9.5 %copy-start.3 = (bf16[8,128,1024]{2,1,0:T(8,128)(2,1)S(1)}, bf16[8,128,1024]{2,1,0:T(8,128)(2,1)}, u32[]{:S(2)}) copy-start(bf16[8,128,1024]{2,1,0:T(8,128)(2,1)} %multiply_convert_fusion.3) | copy-start | bytes 6291460
  189.6 15.7 %copy-start.5 = (bf16[2048,1024]{1,0:T(8,128)(2,1)S(1)}, bf16[2048,1024]{1,0:T(8,128)(2,1)}, u32[]{:S(2)}) copy-start(bf16[2048,1024]{1,0:T(8,128)(2,1)} %copy-done.4) | copy-start | bytes 12582916
  189.6 15.7 %copy-start.7 = (bf16[2048,1024]{1,0:T(8,128)(2,1)S(1)}, bf16[2048,1024]{1,0:T(8,128)(2,1)}, u32[]{:S(2)}) copy-start(bf16[2048,1024]{1,0:T(8,128)(2,1)} %param.19) | copy-start | bytes 12582916
  205.3 668.9 %copy-start.1 = (bf16[1,16,6,128,128]{4,3,2,1,0:T(8,128)(2,1)S(1)}, bf16[1,16,6,128,128]{4,3,2,1,0:T(8,128)(2,1)}, u32[]{:S(2)}) copy-start(bf16[1,16,6,128,128]{4,3,2,1,0:T(8,128)(2,1)} %param.16) | copy-start | bytes 9437188
Sparse Core Ops, SparseCore 0:
  222.9 649.7 reduce-scatter.1
where the time goes:
time: 882 us; the launch traced here: 881 us
  waiting for transfers between devices  724 us (82%)
  matrix products  51.8 us (6%)
  other arithmetic  45.2 us (5%)
  local copies, waits for them, and re-layouts  29.8 us (3%)
  starting transfers between devices  16.3 us (2%)
  between operations  14.2 us (2%)
    reduce_scatter x1, waiting for transfers between devices, on_device(): lax.psum_scatter(lax.dot_general(stacked, delta, (((0,), (0,)), ((), ()))...  650 us
    all_to_all x1, waiting for transfers between devices, on_device(): lax.all_to_all(outgoing, 'dom', split_axis=0, concat_axis=0, tiled=True)  73.7 us
  transfers between devices with their start and end apart: 3, of which 2 were waited for; matrix products, arithmetic and copies ran while one was open for 5% of the time, Pallas kernels for 0%

commit v1 on v0

v1 whole, which is shorter than its diff:
```python
import functools
import math

import jax
import jax.numpy as jnp
from jax import lax
from jax.experimental import pallas as pl
from jax.experimental.pallas import tpu as pltpu
from jax.sharding import PartitionSpec as P

MOMENTUM = 0.6
MESH = pl.DeviceIdType.MESH
BLOCK = 128
FEATS = 1024
PHASES = 4
WIDE = FEATS // PHASES
SLOTS = 16
SUBS = 8
LANES = FEATS // SUBS
F32 = jnp.float32
BF16 = jnp.bfloat16


def place():
    dom = lax.axis_index("dom")
    return dom // 8, lax.rem(dom // 2, 4), lax.rem(dom, 2), lax.axis_index("rep")


def dom_of(z, y, c):
    return (z * 4 + y) * 2 + c


def halo_kernel(
    send_ref, scale_ref, near_ref, own_ref, edge_ref, cache_hbm,
    summed_ref,
    stage, recv, look, cache, cache_sem, send_sem, recv_sem, pass_sem, take_sem,
):
    z, y, c, x = place()
    dom = dom_of(z, y, c)
    right, left = lax.rem(x + 1, 4), lax.rem(x + 3, 4)

    def cache_copy(f):
        return pltpu.make_async_copy(
            cache_hbm.at[:, :, pl.ds(pl.multiple_of(f * WIDE, WIDE), WIDE)], cache.at[f], cache_sem.at[f]
        )

    for f in range(PHASES):
        cache_copy(f).start()

    barrier = pltpu.get_barrier_semaphore()

    @pl.loop(1, 32)
    def _(j):
        to = dom_of(lax.rem(z + j // 8, 4), lax.rem(y + lax.rem(j // 2, 4), 4), lax.rem(c + lax.rem(j, 2), 2))
        pl.semaphore_signal(barrier, inc=1, device_id=(to, x), device_id_type=MESH)

    for to in (right, left):
        pl.semaphore_signal(barrier, inc=1, device_id=(dom, to), device_id_type=MESH)
    pl.semaphore_wait(barrier, 33)

    def offset(i):
        group = lax.rem(x + i // 8, 4)
        t = lax.rem(i, 8)
        dz, dc = t // 2, lax.rem(t, 2)
        dy = lax.rem(group + 4 - dz, 4)
        return group * 8 + t, dz, dy, dc

    def dest(i):
        slot, dz, dy, dc = offset(i)
        return slot, dom_of(lax.rem(z + dz, 4), lax.rem(y + dy, 4), lax.rem(c + dc, 2))

    def fill(f):
        @pl.loop(0, SLOTS)
        def _(i):
            slot, to = dest(i)
            chosen = send_ref[0, to]
            gain = scale_ref[chosen] * MOMENTUM
            cols = pl.ds(pl.multiple_of(f * WIDE, WIDE), WIDE)
            stage[f, i] = (own_ref[chosen, :, cols].astype(F32) * gain).astype(BF16)

    def direct(f, i):
        slot, to = dest(i)
        return slot, pltpu.make_async_remote_copy(
            src_ref=stage.at[f, i], dst_ref=recv.at[f, slot],
            send_sem=send_sem.at[f, i], recv_sem=recv_sem.at[f, i],
            device_id=(to, x), device_id_type=MESH,
        )

    def local(f, i):
        return pltpu.make_async_copy(stage.at[f, i], recv.at[f, 0], recv_sem.at[f, i])

    def start(f, i):
        slot, copy = direct(f, i)

        @pl.when(slot == 0)
        def _():
            local(f, i).start()

        @pl.when(slot != 0)
        def _():
            copy.start()

    def arrive(f, i):
        slot, copy = direct(f, i)

        @pl.when(slot == 0)
        def _():
            local(f, i).wait()

        @pl.when(slot != 0)
        def _():
            copy.wait_recv()

    def onward(f, i):
        slot, _, _, _ = offset(i)
        to = jnp.where(i < 8, right, left)
        return pltpu.make_async_remote_copy(
            src_ref=recv.at[f, slot], dst_ref=recv.at[f, slot],
            send_sem=pass_sem.at[f, i], recv_sem=take_sem.at[f, i],
            device_id=(dom, to), device_id_type=MESH,
        )

    def taken(f, i):
        t = lax.rem(i, 8)
        slot = jnp.where(i < 8, lax.rem(x + 3, 4), lax.rem(x + 2, 4)) * 8 + t
        return pltpu.make_async_remote_copy(
            src_ref=recv.at[f, slot], dst_ref=recv.at[f, slot],
            send_sem=pass_sem.at[f, i], recv_sem=take_sem.at[f, i],
            device_id=(dom, right), device_id_type=MESH,
        )

    def finish(f):
        @pl.loop(0, SLOTS)
        def _(i):
            taken(f, i).wait_recv()

        cache_copy(f).wait()
        cols = pl.ds(pl.multiple_of(f * WIDE, WIDE), WIDE)

        @pl.loop(0, 8)
        def _(b):
            look[b] = (own_ref[b, :, cols].astype(F32) * scale_ref[b]).astype(BF16)

        @pl.loop(0, 32)
        def _(s):
            group, t = s // 8, lax.rem(s, 8)
            dz, dc = t // 2, lax.rem(t, 2)
            dy = lax.rem(group + 4 - dz, 4)
            src = dom_of(lax.rem(z + 4 - dz, 4), lax.rem(y + 4 - dy, 4), lax.rem(c + 2 - dc, 2))
            look[8 + src] = (
                recv[f, s].astype(F32) + (1.0 - MOMENTUM) * cache[f, src].astype(F32)
            ).astype(BF16)

        @pl.loop(0, 16)
        def _(t):
            coefs = jnp.concatenate([edge_ref[t, k] for k in range(6)], axis=1)
            rows = jnp.concatenate([look[near_ref[t, k]] for k in range(6)], axis=0)
            summed_ref[t, :, cols] = jnp.dot(coefs, rows, preferred_element_type=F32).astype(BF16)

    fill(0)

    @pl.loop(0, SLOTS)
    def _(i):
        start(0, i)

    @pl.loop(0, PHASES)
    def _(f):
        @pl.when(f + 1 < PHASES)
        def _():
            fill(f + 1)

        @pl.loop(0, SLOTS)
        def _(i):
            arrive(f, i)
            onward(f, i).start()

            @pl.when(f + 1 < PHASES)
            def _():
                start(f + 1, i)

        @pl.when(f >= 1)
        def _():
            finish(f - 1)

    finish(PHASES - 1)

    @pl.loop(0, PHASES)
    def _(f):
        @pl.loop(0, SLOTS)
        def _(i):
            slot, copy = direct(f, i)

            @pl.when(slot != 0)
            def _():
                copy.wait_send()

            onward(f, i).wait_send()


def exchange(own, scale, cache, send_list, near, edges):
    vmem = pl.BlockSpec(memory_space=pltpu.VMEM)
    smem = pl.BlockSpec(memory_space=pltpu.SMEM)
    return pl.pallas_call(
        halo_kernel,
        out_shape=jax.ShapeDtypeStruct((16, BLOCK, FEATS), BF16),
        in_specs=[smem, smem, smem, vmem, vmem, pl.BlockSpec(memory_space=pl.ANY)],
        out_specs=vmem,
        scratch_shapes=[
            pltpu.VMEM((PHASES, SLOTS, BLOCK, WIDE), BF16),
            pltpu.VMEM((PHASES, 32, BLOCK, WIDE), BF16),
            pltpu.VMEM((40, BLOCK, WIDE), BF16),
            pltpu.VMEM((PHASES, 32, BLOCK, WIDE), BF16),
            pltpu.SemaphoreType.DMA((PHASES,)),
            pltpu.SemaphoreType.DMA((PHASES, SLOTS)),
            pltpu.SemaphoreType.DMA((PHASES, SLOTS)),
            pltpu.SemaphoreType.DMA((PHASES, SLOTS)),
            pltpu.SemaphoreType.DMA((PHASES, SLOTS)),
        ],
        compiler_params=pltpu.CompilerParams(
            collective_id=0, has_side_effects=True, vmem_limit_bytes=56 * 2**20
        ),
        name="halo",
    )(send_list, scale.astype(F32), near, own.reshape(8, BLOCK, FEATS), edges, cache.reshape(32, BLOCK, FEATS))


ORDERS = ((2, 1, 0), (1, 0, 2), (0, 2, 1))


def scatter_kernel(factor, g_ref, out_ref, sent, got0, sum0, got1, sum1, got2, sum2, got3, send_sem, recv_sem):
    z, y, c, x = place()
    at = (z, y, x)

    def mate(axis, off):
        spot = [z, y, x]
        spot[axis] = lax.rem(spot[axis] + off, 4)
        return (dom_of(spot[0], spot[1], c), spot[2])

    other = (dom_of(z, y, 1 - c), x)
    barrier = pltpu.get_barrier_semaphore()
    pl.semaphore_signal(barrier, inc=1, device_id=other, device_id_type=MESH)
    for axis in range(3):
        for off in (1, 2, 3):
            pl.semaphore_signal(barrier, inc=1, device_id=mate(axis, off), device_id_type=MESH)
    pl.semaphore_wait(barrier, 10)

    def copy(src, dst, i, n, to):
        return pltpu.make_async_remote_copy(
            src_ref=src, dst_ref=dst, send_sem=send_sem.at[i, n], recv_sem=recv_sem.at[i, n],
            device_id=to, device_id_type=MESH,
        )

    def pick(ref, i, dims, axis, index):
        return ref.at[(i,) + tuple(index if d == axis else slice(None) for d in dims)]

    def load(ref, i, dims, axis, index):
        return ref[(i,) + tuple(index if d == axis else slice(None) for d in dims)]

    def cross(i):
        return copy(sent.at[i, 1 - c], got0.at[i], i, 0, other)

    def hop(i, stage, off):
        order = ORDERS[i % 3]
        axis = order[stage]
        dims = [d for d in (0, 1, 2) if d not in order[:stage]]
        src = (sum0, sum1, sum2)[stage]
        dst = (got1, got2, got3)[stage]
        goal = lax.rem(at[axis] + off, 4)
        return copy(pick(src, i, dims, axis, goal), dst.at[i, off - 1], i, 1 + 3 * stage + off - 1, mate(axis, off))

    def total(i, stage):
        order = ORDERS[i % 3]
        axis = order[stage]
        dims = [d for d in (0, 1, 2) if d not in order[:stage]]
        src = (sum0, sum1, sum2)[stage]
        dst = (got1, got2, got3)[stage]
        part = load(src, i, dims, axis, at[axis]).astype(F32)
        for off in range(3):
            part = part + dst[i, off].astype(F32)
        return part

    def make(i):
        part = g_ref[:, i * LANES:(i + 1) * LANES].astype(BF16).reshape(4, 4, 2, 4, 16, LANES)
        sent[i, 0] = part[:, :, 0]
        sent[i, 1] = part[:, :, 1]

    def step(i, stage):
        if stage == 0:
            make(i)
            cross(i).start()
        elif stage == 1:
            cross(i).wait_recv()
            sum0[i] = (sent[i, c].astype(F32) + got0[i].astype(F32)).astype(BF16)
            for off in (1, 2, 3):
                hop(i, 0, off).start()
        elif stage < 4:
            for off in (1, 2, 3):
                hop(i, stage - 2, off).wait_recv()
            (sum1, sum2)[stage - 2][i] = total(i, stage - 2).astype(BF16)
            for off in (1, 2, 3):
                hop(i, stage - 1, off).start()
        else:
            for off in (1, 2, 3):
                hop(i, 2, off).wait_recv()
            out_ref[:, i * LANES:(i + 1) * LANES] = total(i, 2) * factor

    for tick in range(SUBS + 4):
        for stage in (4, 3, 2, 1, 0):
            i = tick - stage
            if 0 <= i < SUBS:
                step(i, stage)

    for i in range(SUBS):
        cross(i).wait_send()
        for stage in range(3):
            for off in (1, 2, 3):
                hop(i, stage, off).wait_send()


def scatter(grads, factor):
    vmem = pl.BlockSpec(memory_space=pltpu.VMEM)
    return pl.pallas_call(
        functools.partial(scatter_kernel, factor),
        out_shape=jax.ShapeDtypeStruct((16, FEATS), F32),
        in_specs=[vmem],
        out_specs=vmem,
        scratch_shapes=[
            pltpu.VMEM((SUBS, 2, 4, 4, 4, 16, LANES), BF16),
            pltpu.VMEM((SUBS, 4, 4, 4, 16, LANES), BF16),
            pltpu.VMEM((SUBS, 4, 4, 4, 16, LANES), BF16),
            pltpu.VMEM((SUBS, 3, 4, 4, 16, LANES), BF16),
            pltpu.VMEM((SUBS, 4, 4, 16, LANES), BF16),
            pltpu.VMEM((SUBS, 3, 4, 16, LANES), BF16),
            pltpu.VMEM((SUBS, 4, 16, LANES), BF16),
            pltpu.VMEM((SUBS, 3, 16, LANES), BF16),
            pltpu.SemaphoreType.DMA((SUBS, 10)),
            pltpu.SemaphoreType.DMA((SUBS, 10)),
        ],
        compiler_params=pltpu.CompilerParams(
            collective_id=1, has_side_effects=True, vmem_limit_bytes=56 * 2**20
        ),
        name="scatter",
    )(grads)


def on_device(
    own_values, own_scale, halo_cache, send_list, batch_ids, neighbor_blocks, edge_tiles, w_self, w_neigh, cotangent,
):
    summed = exchange(own_values, own_scale, halo_cache, send_list, neighbor_blocks[0], edge_tiles[0])
    own_blocks = own_values.reshape(8, BLOCK, FEATS)
    own_deq = (own_blocks.astype(F32) * own_scale.astype(F32)[:, None, None]).astype(BF16)
    self_flat = jnp.take(own_deq, batch_ids[0], axis=0).reshape(-1, FEATS)
    summed_flat = summed.reshape(-1, FEATS)
    pre_act = jnp.dot(self_flat, w_self, preferred_element_type=F32) + jnp.dot(
        summed_flat, w_neigh, preferred_element_type=F32
    )
    sigmoid_z = jax.nn.sigmoid(pre_act)
    output_rows = (pre_act * sigmoid_z).astype(BF16)
    delta = (cotangent.astype(F32) * sigmoid_z * (1.0 + pre_act * (1.0 - sigmoid_z))).astype(BF16)
    stacked = jnp.concatenate([self_flat, summed_flat], axis=1)
    grads = lax.dot_general(stacked, delta, (((0,), (0,)), ((), ())), preferred_element_type=F32)
    rows = stacked.shape[0] * lax.axis_size("dom") * lax.axis_size("rep")
    return output_rows, scatter(grads, 1.0 / math.sqrt(rows))


def solution(mesh):
    placed = (
        P("dom", None), P("dom"), P("dom", None), P("dom", None), P("dom", "rep"), P("dom", "rep", None),
        P("dom", "rep", None, None, None), P(), P(), P(("dom", "rep"), None),
    )
    return jax.shard_map(
        on_device,
        mesh=mesh,
        in_specs=placed,
        out_specs=(P(("dom", "rep"), None), P(("dom", "rep"), None)),
        check_vma=False,
    )
```

time: 882 us -> 193 us (0.22)
  waiting for transfers between devices: 724 us -> 0 us
  Pallas kernels: 0 us -> 147 us
  other arithmetic: 45.2 us -> 8.43 us
  matrix products: 51.8 us -> 28.8 us
  local copies, waits for them, and re-layouts: 29.8 us -> 7.34 us
  starting transfers between devices: 16.3 us -> 0 us
  between operations: 14.2 us -> 0.7 us
    reduce_scatter x1 -> x0, waiting for transfers between devices: 650 us -> none  [on_device(): lax.psum_scatter(lax.dot_general(stacked, delta, (((0,), (0,)), ((), ()))...]
    pallas_call x0 -> x2, Pallas kernels: none -> 147 us  [the longest x1 80.9 us: exchange(): pl.pallas_call(halo_kernel, out_shape=jax.ShapeDtypeStruct((16, BLOCK, FE...]
    all_to_all x2 -> x0, waiting for transfers between devices: 73.7 us -> none  [the longest x1 73.7 us: on_device(): lax.all_to_all(outgoing, 'dom', split_axis=0, concat_axis=0, tiled=True)]
    gather x4 -> x1, local copies, waits for them, and re-layouts: 26.6 us -> 4.42 us  [on_device(): self_flat = jnp.take(own_deq, batch_ids[0], axis=0).reshape(-1, FEATS)]
    dot_general x3 -> x2, matrix products: 34.4 us -> 14.4 us  [the longest x1 8.15 us: on_device(): jnp.dot(summed_flat, w_neigh, preferred_element_type=F32)]
    all_to_all x2 -> x0, starting transfers between devices: 16.1 us -> none  [the longest x1 8.42 us: on_device(): lax.all_to_all(out_scale, 'dom', split_axis=0, concat_axis=0, tiled=True)]
    mul x3 -> x0, other arithmetic: 13.3 us -> none  [the longest x1 11.5 us: on_device(): (1.0 - MOMENTUM) * caches.astype(jnp.float32)]
  transfers between devices with their start and end apart: 3 -> 0, of which waited for: 2 -> 0; matrix products, arithmetic and copies ran while one was open for 5% -> 0% of each run, Pallas kernels for 0% -> 0%
where the time goes in v1:
time: 193 us; the launch traced here: 192 us
  Pallas kernels  147 us (76%)
  matrix products  28.8 us (15%)
  other arithmetic  8.43 us (4%)
  local copies, waits for them, and re-layouts  7.34 us (4%)
    pallas_call x1, Pallas kernels, exchange(): pl.pallas_call(halo_kernel, out_shape=jax.ShapeDtypeStruct((16, BLOCK, FE...  80.9 us
    pallas_call x1, Pallas kernels, scatter(): pl.pallas_call(functools.partial(scatter_kernel, factor), out_shape=jax.S...  66.2 us
    dot_general x1, matrix products, on_device(): lax.dot_general(stacked, delta, (((0,), (0,)), ((), ())), preferred_eleme...  14.4 us
    dot_general x1, matrix products, on_device(): jnp.dot(summed_flat, w_neigh, preferred_element_type=F32)  8.15 us
    dot_general x1, matrix products, on_device(): jnp.dot(self_flat, w_self, preferred_element_type=F32)  6.27 us
    gather x1, local copies, waits for them, and re-layouts, on_device(): self_flat = jnp.take(own_deq, batch_ids[0], axis=0).reshape(-1, FEATS)  4.42 us

profile of v1, /device:TPU:0, one launch (start us, length us, event | category | flops | bytes accessed | tf_op | source)
XLA Modules:
  0.0 192.5 jit_solution(13898396663063397062)
XLA Ops:
  0.6 0.0 copy-start
  0.6 0.8 convert_element_type.20.scale_ref
  1.5 0.0 copy-start.2
  1.5 0.7 fusion.5
  2.1 0.7 compare_and_fusion
  2.8 0.1 broadcast_bitcast_fusion
  2.9 1.4 copy.13
  4.2 3.8 %multiply_convert_fusion.3 = bf16[8,128,1024]{2,1,0:T(8,128)(2,1)} fusion(bf16[8,128,1024]{2,1,0:T(8,128)(2,1)} %bitcast.20, f32[8]{0:T(128)S(1)} %convert_element_type.20.scale_ref), kind=kLoop, calls=%fused_computation.10 | loop fusion | flops 3145728 | bytes 4194336 | tf_op jit(solution)/shard_map/convert_element_type | solution.py:350
  8.0 4.4 %gather_fusion = bf16[16,128,1024]{2,1,0:T(8,128)(2,1)} fusion(bf16[8,128,1024]{2,1,0:T(8,128)(2,1)} %multiply_convert_fusion.3, s32[1024]{0:T(1024)S(1)} %pad_clamp_fusion), kind=kCustom, calls=%fused_computation | custom fusion | bytes 8388672 | tf_op jit(solution)/shard_map/jit(_take)/gather | solution.py:351
  12.4 0.0 copy-done.2
  12.4 2.5 %bitcast_select_fusion = bf16[2048,1024]{1,0:T(8,128)(2,1)S(1)} fusion(bf16[16,128,1024]{2,1,0:T(8,128)(2,1)} %gather_fusion, pred[2048]{0:T(1024)(128)(4,1)S(1)} %broadcast_bitcast_fusion), kind=kLoop, calls=%fused_computation.8 | loop fusion | flops 2097152 | bytes 8390656 | tf_op jit(solution)/shard_map/jit(_take)/select_n | solution.py:351
  14.9 80.9 %halo.1 = bf16[16,128,1024]{2,1,0:T(8,128)(2,1)} custom-call(s32[1,32]{1,0:T(1,128)} %send_ref.1, f32[8]{0:T(128)} %copy-done.2, s32[16,6]{1,0:T(8,128)} %bitcast.25, bf16[8,128,1024]{2,1,0:T(8,128)(2,1)} %bitcast.21, bf16[16,6,128,128]{3,2,1,0:T(8,128)(2,1)} %bitcast.24, bf16[32,128,1024]{2,1,0:T(8,128)(2,1)} %bitcast.19), custom_call_target="tpu_custom_call" | custom-call | tf_op jit(solution)/shard_map/halo/pallas_call | solution.py:203
  95.9 0.0 copy-start.1
  95.9 6.3 %fusion.8 = f32[2048,1024]{1,0:T(8,128)S(1)} fusion(bf16[2048,1024]{1,0:T(8,128)(2,1)S(1)} %bitcast_select_fusion, bf16[1024,1024]{1,0:T(8,128)(2,1)} %param.17), kind=kOutput, calls=%fused_computation.20 | convolution fusion | flops 4294967296 | bytes 14680064 | tf_op jit(solution)/shard_map/dot_general | solution.py:353
  102.1 0.0 copy-done
  102.2 0.0 copy-done.1
  102.2 8.2 %multiply_convert_fusion.1 = (bf16[2048,1024]{1,0:T(8,128)(2,1)}, f32[2048,1024]{1,0:T(8,128)}) fusion(f32[2048,1024]{1,0:T(8,128)S(1)} %fusion.8, bf16[2048,1024]{1,0:T(8,128)(2,1)S(1)} %bitcast.22, bf16[1024,1024]{1,0:T(8,128)(2,1)S(1)} %copy-done), kind=kOutput, calls=%fused_computation.6 | convolution fusion | flops 4307550208 | bytes 27262976 | tf_op jit(solution)/shard_map/dot_general | solution.py:353
  110.3 14.4 %fusion.g_ref = f32[2048,1024]{1,0:T(8,128)} fusion(bf16[2048,1024]{1,0:T(8,128)(2,1)S(1)} %bitcast.23, bf16[2048,1024]{1,0:T(8,128)(2,1)S(1)} %bitcast_select_fusion, f32[2048,1024]{1,0:T(8,128)} %get-tuple-element.3, bf16[2048,1024]{1,0:T(8,128)(2,1)} %param.19), kind=kOutput, calls=%fused_computation.1 | convolution fusion | flops 8627683328 | bytes 29360128 | tf_op jit(solution)/shard_map/dot_general | solution.py:360
  124.7 66.2 %scatter.1 = f32[16,1024]{1,0:T(8,128)} custom-call(f32[2048,1024]{1,0:T(8,128)} %fusion.g_ref), custom_call_target="tpu_custom_call" | custom-call | tf_op jit(solution)/shard_map/scatter/pallas_call | solution.py:321
  191.0 1.5 copy.15
  (1 shorter events, 0.0 us)
Async XLA Ops:
  0.6 101.5 %copy-start = (bf16[1024,1024]{1,0:T(8,128)(2,1)S(1)}, bf16[1024,1024]{1,0:T(8,128)(2,1)}, u32[]{:S(2)}) copy-start(bf16[1024,1024]{1,0:T(8,128)(2,1)} %param.18) | copy-start | bytes 6291460
  1.5 11.0 %copy-start.2 = (f32[8]{0:T(128)}, f32[8]{0:T(128)S(1)}, u32[]{:S(2)}) copy-start(f32[8]{0:T(128)S(1)} %convert_element_type.20.scale_ref) | copy-start | bytes 100
  95.9 6.3 %copy-start.1 = (bf16[16,128,1024]{2,1,0:T(8,128)(2,1)S(1)}, bf16[16,128,1024]{2,1,0:T(8,128)(2,1)}, u32[]{:S(2)}) copy-start(bf16[16,128,1024]{2,1,0:T(8,128)(2,1)} %halo.1) | copy-start | bytes 12582916

commit v2 on v0

v2 whole, which is shorter than its diff:
```python
import functools
import math

import jax
import jax.numpy as jnp
from jax import lax
from jax.experimental import pallas as pl
from jax.experimental.pallas import tpu as pltpu
from jax.sharding import PartitionSpec as P

MOMENTUM = 0.6
MESH = pl.DeviceIdType.MESH
BLOCK = 128
FEATS = 1024
PHASES = 4
WIDE = FEATS // PHASES
PAIRS = 8
LANES = 128
TARGETS = 16
PIECE = (2, 4, 16, WIDE)
F32 = jnp.float32
BF16 = jnp.bfloat16
ORDERS = ((2, 1, 0), (1, 0, 2), (0, 2, 1))


def dom_of(z, y, c):
    return (z * 4 + y) * 2 + c


def columns(f):
    return pl.ds(pl.multiple_of(f * WIDE, WIDE), WIDE)


def layer_kernel(
    factor,
    send_ref, scale_ref, near_ref, self_ref, own_hbm, edge_hbm, cache_hbm, wself_hbm, wneigh_hbm, cot_hbm,
    out_hbm, grad_ref,
    own, edge, wself, wneigh, cache, cot, outs, deq, deq_t, base, look, acc, summed_t, delta,
    pool, recv, xfer, got0, got1, sum1, got2, sum2, got3,
    load_sem, cache_sem, cot_sem, out_sem,
    send_sem, recv_sem, swap_out, swap_in, pass_sem, take_sem, cross_out, cross_in, hop_out, hop_in,
):
    dom, x = lax.axis_index("dom"), lax.axis_index("rep")
    z, y, c = dom // 8, lax.rem(dom // 2, 4), lax.rem(dom, 2)
    right, left = lax.rem(x + 1, 4), lax.rem(x + 3, 4)
    other = (dom_of(z, y, 1 - c), x)

    loads = [
        pltpu.make_async_copy(src, dst, load_sem.at[n])
        for n, (src, dst) in enumerate(((own_hbm, own), (wself_hbm, wself), (wneigh_hbm, wneigh), (edge_hbm, edge)))
    ]

    def cache_copy(f):
        s = lax.rem(f, 2)
        return pltpu.make_async_copy(cache_hbm.at[:, :, columns(f)], cache.at[s], cache_sem.at[s])

    def cot_copy(n):
        return pltpu.make_async_copy(cot_hbm.at[:, :, columns(n)], cot.at[n % 2], cot_sem.at[n % 2])

    def out_copy(n):
        return pltpu.make_async_copy(outs.at[n % 2], out_hbm.at[:, :, columns(n)], out_sem.at[n % 2])

    for load in loads:
        load.start()
    for n in range(2):
        cache_copy(n).start()
        cot_copy(n).start()

    barrier = pltpu.get_barrier_semaphore()

    @pl.loop(1, 16)
    def _(j):
        to = dom_of(lax.rem(z + j // 4, 4), lax.rem(y + lax.rem(j, 4), 4), c)
        pl.semaphore_signal(barrier, inc=1, device_id=(to, x), device_id_type=MESH)

    @pl.loop(1, 4)
    def _(j):
        pl.semaphore_signal(barrier, inc=1, device_id=(dom, lax.rem(x + j, 4)), device_id_type=MESH)

    pl.semaphore_signal(barrier, inc=1, device_id=other, device_id_type=MESH)

    def offset(i):
        group, dz = lax.rem(x + lax.rem(i, 2), 4), i // 2
        return group, dz, lax.rem(group + 4 - dz, 4)

    def slot_of(group, dz, dc):
        return group * 8 + dz * 2 + dc

    def staged(f, i, w):
        return pool.at[f, i // 4, lax.rem(i, 4), pl.ds(2 * w, 2)]

    def handed(f, i):
        return xfer.at[f, i // 2, pl.ds(2 * lax.rem(i, 2), 2)]

    def fill(f):
        @pl.loop(0, PAIRS)
        def _(i):
            _, dz, dy = offset(i)
            for w in range(2):
                core = c if w == 0 else 1 - c
                chosen = send_ref[0, dom_of(lax.rem(z + dz, 4), lax.rem(y + dy, 4), core)]
                gain = scale_ref[chosen] * MOMENTUM
                rows = (own[chosen, :, columns(f)].astype(F32) * gain).astype(BF16)
                pool[f, i // 4, lax.rem(i, 4), pl.ds(2 * w, 2)] = rows.reshape(PIECE)

    def target(f, i, w):
        group, dz, _ = offset(i)
        return recv.at[f, slot_of(group, dz, 0)] if w == 0 else handed(f, i)

    def direct(f, i, w):
        _, dz, dy = offset(i)
        return pltpu.make_async_remote_copy(
            src_ref=staged(f, i, w), dst_ref=target(f, i, w),
            send_sem=send_sem.at[f, i, w], recv_sem=recv_sem.at[f, i, w],
            device_id=(dom_of(lax.rem(z + dz, 4), lax.rem(y + dy, 4), c), x), device_id_type=MESH,
        )

    def local(f, i, w):
        return pltpu.make_async_copy(staged(f, i, w), target(f, i, w), recv_sem.at[f, i, w])

    def stays(i):
        group, dz, _ = offset(i)
        return group * 4 + dz == 0

    def start(f, i):
        @pl.when(stays(i))
        def _():
            for w in range(2):
                local(f, i, w).start()

        @pl.when(jnp.logical_not(stays(i)))
        def _():
            for w in range(2):
                direct(f, i, w).start()

    def arrive(f, i, w):
        @pl.when(stays(i))
        def _():
            local(f, i, w).wait()

        @pl.when(jnp.logical_not(stays(i)))
        def _():
            direct(f, i, w).wait_recv()

    def swap(f, i):
        group, dz, _ = offset(i)
        return pltpu.make_async_remote_copy(
            src_ref=handed(f, i), dst_ref=recv.at[f, slot_of(group, dz, 1)],
            send_sem=swap_out.at[f, i], recv_sem=swap_in.at[f, i],
            device_id=other, device_id_type=MESH,
        )

    def onward(f, i, dc):
        group, dz, _ = offset(i)
        slot = slot_of(group, dz, dc)
        return pltpu.make_async_remote_copy(
            src_ref=recv.at[f, slot], dst_ref=recv.at[f, slot],
            send_sem=pass_sem.at[f, i, dc], recv_sem=take_sem.at[f, i, dc],
            device_id=(dom, jnp.where(lax.rem(i, 2) == 0, right, left)), device_id_type=MESH,
        )

    def taken(f, i, dc):
        group = lax.rem(x + 3 - lax.rem(i, 2), 4)
        slot = slot_of(group, i // 2, dc)
        return pltpu.make_async_remote_copy(
            src_ref=recv.at[f, slot], dst_ref=recv.at[f, slot],
            send_sem=pass_sem.at[f, i, dc], recv_sem=take_sem.at[f, i, dc],
            device_id=(dom, right), device_id_type=MESH,
        )

    def after_swap(f, i):
        swap(f, i).wait_recv()
        onward(f, i, 1).start()

    def prepare():
        @pl.loop(0, 8)
        def _(b):
            rows = (own[b].astype(F32) * scale_ref[b]).astype(BF16)
            deq[b] = rows
            deq_t[b] = rows.T

        loads[1].wait()

        @pl.loop(0, PHASES)
        def _(n):
            base[...] = jnp.dot(
                deq[...].reshape(FEATS, FEATS), wself[:, columns(n)], preferred_element_type=F32
            ).reshape(8, BLOCK, WIDE)

            @pl.loop(0, TARGETS)
            def _(t):
                acc[t, :, columns(n)] = base[self_ref[0, t]]

        loads[2].wait()
        loads[3].wait()

    def finish(f):
        @pl.loop(0, PAIRS)
        def _(i):
            for dc in range(2):
                taken(f, i, dc).wait_recv()

        cache_copy(f).wait()

        @pl.loop(0, 8)
        def _(b):
            look[b] = deq[b, :, columns(f)]

        @pl.loop(0, 32)
        def _(s):
            group, dz, dc = s // 8, lax.rem(s, 8) // 2, lax.rem(s, 2)
            dy = lax.rem(group + 4 - dz, 4)
            src = dom_of(lax.rem(z + 4 - dz, 4), lax.rem(y + 4 - dy, 4), lax.rem(c + dc, 2))
            fresh = recv[f, s].reshape(BLOCK, WIDE).astype(F32)
            look[8 + src] = (fresh + (1.0 - MOMENTUM) * cache[lax.rem(f, 2), src].astype(F32)).astype(BF16)

        @pl.when(f + 2 < PHASES)
        def _():
            cache_copy(f + 2).start()

        @pl.loop(0, 4)
        def _(g):
            parts = []
            for q in range(4):
                t = 4 * g + q
                coefs = jnp.concatenate([edge[t, k] for k in range(6)], axis=1)
                rows = jnp.concatenate([look[near_ref[t, k]] for k in range(6)], axis=0)
                part = jnp.dot(coefs, rows, preferred_element_type=F32).astype(BF16)
                summed_t[t, columns(f), :] = part.T
                parts.append(part)
            whole = jnp.concatenate(parts, axis=0)
            for n in range(PHASES):
                cols = slice(n * WIDE, (n + 1) * WIDE)
                more = jnp.dot(whole, wneigh[columns(f), cols], preferred_element_type=F32)
                acc[pl.ds(4 * g, 4), :, cols] += more.reshape(4, BLOCK, WIDE)

    loads[0].wait()
    fill(0)
    pl.semaphore_wait(barrier, 19)

    @pl.loop(0, PAIRS)
    def _(i):
        start(0, i)

    @pl.loop(0, PHASES)
    def _(f):
        @pl.when(f + 1 < PHASES)
        def _():
            fill(f + 1)

        @pl.loop(0, PAIRS)
        def _(i):
            arrive(f, i, 0)
            onward(f, i, 0).start()
            arrive(f, i, 1)
            swap(f, i).start()

            @pl.when(f + 1 < PHASES)
            def _():
                start(f + 1, i)

            @pl.when(i >= 1)
            def _():
                after_swap(f, i - 1)

        after_swap(f, PAIRS - 1)

        @pl.when(f == 0)
        def _():
            prepare()

        @pl.when(f >= 1)
        def _():
            finish(f - 1)

    finish(PHASES - 1)

    @pl.loop(0, PHASES)
    def _(f):
        @pl.loop(0, PAIRS)
        def _(i):
            @pl.when(jnp.logical_not(stays(i)))
            def _():
                for w in range(2):
                    direct(f, i, w).wait_send()

            swap(f, i).wait_send()

    at = (z, y, x)

    def mate(axis, off):
        spot = [z, y, x]
        spot[axis] = lax.rem(spot[axis] + off, 4)
        return (dom_of(spot[0], spot[1], c), spot[2])

    def cross(n, zz):
        return pltpu.make_async_remote_copy(
            src_ref=pool.at[n, 1 - c, zz], dst_ref=got0.at[n, zz],
            send_sem=cross_out.at[n, zz], recv_sem=cross_in.at[n, zz],
            device_id=other, device_id_type=MESH,
        )

    def plan(i, stage):
        order = ORDERS[i % 3]
        axis = order[stage]
        dims = [d for d in (0, 1, 2) if d not in order[:stage]]
        return axis, dims

    def hop(i, stage, off):
        axis, dims = plan(i, stage)
        goal = lax.rem(at[axis] + off, 4)
        cut = tuple(goal if d == axis else slice(None) for d in dims)
        if stage == 0:
            src = xfer.at[(i // 2,) + cut + (slice(None), pl.ds(i % 2 * LANES, LANES))]
        else:
            src = (sum1, sum2)[stage - 1].at[(i,) + cut]
        return pltpu.make_async_remote_copy(
            src_ref=src, dst_ref=(got1, got2, got3)[stage].at[i, off - 1],
            send_sem=hop_out.at[i, stage, off - 1], recv_sem=hop_in.at[i, stage, off - 1],
            device_id=mate(axis, off), device_id_type=MESH,
        )

    def total(i, stage):
        axis, dims = plan(i, stage)
        cut = tuple(at[axis] if d == axis else slice(None) for d in dims)
        if stage == 0:
            part = xfer[(i // 2,) + cut + (slice(None), slice(i % 2 * LANES, (i % 2 + 1) * LANES))]
        else:
            part = (sum1, sum2)[stage - 1][(i,) + cut]
        part = part.astype(F32)
        for off in range(3):
            part = part + (got1, got2, got3)[stage][i, off].astype(F32)
        return part

    def step(n, stage):
        if stage == 0:
            for zz in range(4):
                cross(n, zz).wait_recv()
                xfer[n, zz] = (pool[n, c, zz].astype(F32) + got0[n, zz].astype(F32)).astype(BF16)
        for i in (2 * n, 2 * n + 1):
            if stage > 0:
                for off in (1, 2, 3):
                    hop(i, stage - 1, off).wait_recv()
                part = total(i, stage - 1)
                if stage < 3:
                    (sum1, sum2)[stage - 1][i] = part.astype(BF16)
                else:
                    grad_ref[:, i * LANES:(i + 1) * LANES] = part * factor
            if stage < 3:
                for off in (1, 2, 3):
                    hop(i, stage, off).start()

    def activate(n, t):
        pre = acc[t, :, n * WIDE:(n + 1) * WIDE]
        gate = jax.nn.sigmoid(pre)
        outs[n % 2, t] = (pre * gate).astype(BF16)
        delta[n % 2, t] = (cot[n % 2, t].astype(F32) * gate * (1.0 + pre * (1.0 - gate))).astype(BF16)

    def before(n):
        cot_copy(n).wait()
        if n >= 2:
            out_copy(n - 2).wait()

    def after(n):
        out_copy(n).start()
        if n + 2 < PHASES:
            cot_copy(n + 2).start()

    before(0)

    @pl.loop(0, TARGETS)
    def _(t):
        activate(0, t)

    after(0)

    for n in range(PHASES):
        if n + 1 < PHASES:
            before(n + 1)
        for half in range(2):
            @pl.loop(0, 2)
            def _(m):
                rows = pl.ds(pl.multiple_of(m * 512, 512), 512)
                if half == 0:
                    lhs = [deq_t[self_ref[0, t], rows, :] for t in range(TARGETS)]
                else:
                    lhs = [summed_t[t, rows, :] for t in range(TARGETS)]
                part = jnp.dot(
                    jnp.concatenate(lhs, axis=1), delta[n % 2].reshape(TARGETS * BLOCK, WIDE),
                    preferred_element_type=F32,
                ).astype(BF16).reshape(4, 2, 4, 16, WIDE)
                zz = 2 * half + m
                for core in range(2):
                    pool[n, core, zz] = part[:, core]
                cross(n, zz).start()
                if n + 1 < PHASES:
                    for q in range(4):
                        activate(n + 1, 4 * zz + q)

            if half == 0:
                for stage in (3, 2, 1, 0):
                    if 0 <= n - 1 - stage:
                        step(n - 1 - stage, stage)
        if n + 1 < PHASES:
            after(n + 1)

    for tick in range(PHASES, PHASES + 4):
        for stage in (3, 2, 1, 0):
            if 0 <= tick - 1 - stage < PHASES:
                step(tick - 1 - stage, stage)

    out_copy(PHASES - 2).wait()
    out_copy(PHASES - 1).wait()

    @pl.loop(0, PHASES)
    def _(f):
        @pl.loop(0, PAIRS)
        def _(i):
            for dc in range(2):
                onward(f, i, dc).wait_send()

        @pl.loop(0, 4)
        def _(zz):
            cross(f, zz).wait_send()

    for i in range(2 * PHASES):
        for stage in range(3):
            for off in (1, 2, 3):
                hop(i, stage, off).wait_send()


def layer(factor, send_list, scale, near, batch, own, edges, cache, w_self, w_neigh, cot):
    vmem = pl.BlockSpec(memory_space=pltpu.VMEM)
    smem = pl.BlockSpec(memory_space=pltpu.SMEM)
    hbm = pl.BlockSpec(memory_space=pl.ANY)
    subs = 2 * PHASES
    dma = pltpu.SemaphoreType.DMA
    return pl.pallas_call(
        functools.partial(layer_kernel, factor),
        out_shape=(
            jax.ShapeDtypeStruct((TARGETS, BLOCK, FEATS), BF16),
            jax.ShapeDtypeStruct((16, FEATS), F32),
        ),
        in_specs=[smem] * 4 + [hbm] * 6,
        out_specs=(hbm, vmem),
        scratch_shapes=[
            pltpu.VMEM((8, BLOCK, FEATS), BF16),
            pltpu.VMEM((TARGETS, 6, BLOCK, BLOCK), BF16),
            pltpu.VMEM((FEATS, FEATS), BF16),
            pltpu.VMEM((FEATS, FEATS), BF16),
            pltpu.VMEM((2, 32, BLOCK, WIDE), BF16),
            pltpu.VMEM((2, TARGETS, BLOCK, WIDE), BF16),
            pltpu.VMEM((2, TARGETS, BLOCK, WIDE), BF16),
            pltpu.VMEM((8, BLOCK, FEATS), BF16),
            pltpu.VMEM((8, FEATS, BLOCK), BF16),
            pltpu.VMEM((8, BLOCK, WIDE), F32),
            pltpu.VMEM((40, BLOCK, WIDE), BF16),
            pltpu.VMEM((TARGETS, BLOCK, FEATS), F32),
            pltpu.VMEM((TARGETS, FEATS, BLOCK), BF16),
            pltpu.VMEM((2, TARGETS, BLOCK, WIDE), BF16),
            pltpu.VMEM((PHASES, 2, 4, 4, 4, 16, WIDE), BF16),
            pltpu.VMEM((PHASES, 32) + PIECE, BF16),
            pltpu.VMEM((PHASES, 4, 4, 4, 16, WIDE), BF16),
            pltpu.VMEM((PHASES, 4, 4, 4, 16, WIDE), BF16),
            pltpu.VMEM((subs, 3, 4, 4, 16, LANES), BF16),
            pltpu.VMEM((subs, 4, 4, 16, LANES), BF16),
            pltpu.VMEM((subs, 3, 4, 16, LANES), BF16),
            pltpu.VMEM((subs, 4, 16, LANES), BF16),
            pltpu.VMEM((subs, 3, 16, LANES), BF16),
            dma((4,)), dma((2,)), dma((2,)), dma((2,)),
            dma((PHASES, PAIRS, 2)), dma((PHASES, PAIRS, 2)), dma((PHASES, PAIRS)), dma((PHASES, PAIRS)),
            dma((PHASES, PAIRS, 2)), dma((PHASES, PAIRS, 2)), dma((PHASES, 4)), dma((PHASES, 4)),
            dma((subs, 3, 3)), dma((subs, 3, 3)),
        ],
        compiler_params=pltpu.CompilerParams(
            collective_id=0, has_side_effects=True, vmem_limit_bytes=62 * 2**20
        ),
        name="layer",
    )(send_list, scale, near, batch, own, edges, cache, w_self, w_neigh, cot)


def on_device(
    own_values, own_scale, halo_cache, send_list, batch_ids, neighbor_blocks, edge_tiles, w_self, w_neigh, cotangent,
):
    rows = cotangent.shape[0] * lax.axis_size("dom") * lax.axis_size("rep")
    output_rows, grads = layer(
        1.0 / math.sqrt(rows), send_list, own_scale.astype(F32), neighbor_blocks[0], batch_ids,
        own_values.reshape(8, BLOCK, FEATS), edge_tiles[0], halo_cache.reshape(32, BLOCK, FEATS),
        w_self, w_neigh, cotangent.reshape(TARGETS, BLOCK, FEATS),
    )
    return output_rows.reshape(-1, FEATS), grads


def solution(mesh):
    placed = (
        P("dom", None), P("dom"), P("dom", None), P("dom", None), P("dom", "rep"), P("dom", "rep", None),
        P("dom", "rep", None, None, None), P(), P(), P(("dom", "rep"), None),
    )
    return jax.shard_map(
        on_device,
        mesh=mesh,
        in_specs=placed,
        out_specs=(P(("dom", "rep"), None), P(("dom", "rep"), None)),
        check_vma=False,
    )
```

time: 882 us -> 126 us (0.14)
  waiting for transfers between devices: 724 us -> 0 us
  Pallas kernels: 0 us -> 118 us
  matrix products: 51.8 us -> 0 us
  other arithmetic: 45.2 us -> 1.17 us
  local copies, waits for them, and re-layouts: 29.8 us -> 6.66 us
  starting transfers between devices: 16.3 us -> 0 us
  between operations: 14.2 us -> 0.65 us
    reduce_scatter x1 -> x0, waiting for transfers between devices: 650 us -> none  [on_device(): lax.psum_scatter(lax.dot_general(stacked, delta, (((0,), (0,)), ((), ()))...]
    pallas_call x0 -> x1, Pallas kernels: none -> 118 us  [layer(): pl.pallas_call(functools.partial(layer_kernel, factor), out_shape=(jax.Sh...]
    all_to_all x2 -> x0, waiting for transfers between devices: 73.7 us -> none  [the longest x1 73.7 us: on_device(): lax.all_to_all(outgoing, 'dom', split_axis=0, concat_axis=0, tiled=True)]
    dot_general x4 -> x0, matrix products: 51.8 us -> none  [the longest x1 17.4 us: on_device(): lax.dot_general(stacked, delta, (((0,), (0,)), ((), ())), preferred_eleme...]
    gather x4 -> x0, local copies, waits for them, and re-layouts: 26.6 us -> none  [the longest x1 14.2 us: on_device(): gathered = jnp.take(lookup, neighbor_blocks[0], axis=0)]
    all_to_all x2 -> x0, starting transfers between devices: 16.1 us -> none  [the longest x1 8.42 us: on_device(): lax.all_to_all(out_scale, 'dom', split_axis=0, concat_axis=0, tiled=True)]
    mul x3 -> x0, other arithmetic: 13.3 us -> none  [the longest x1 11.5 us: on_device(): (1.0 - MOMENTUM) * caches.astype(jnp.float32)]
    convert_element_type x3 -> x1, other arithmetic: 13.3 us -> 1.17 us  [on_device(): own_scale.astype(F32)]
  transfers between devices with their start and end apart: 3 -> 0, of which waited for: 2 -> 0; matrix products, arithmetic and copies ran while one was open for 5% -> 0% of each run, Pallas kernels for 0% -> 0%
where the time goes in v2:
time: 126 us
  Pallas kernels  118 us (94%)
  local copies, waits for them, and re-layouts  6.66 us (5%)
    pallas_call x1, Pallas kernels, layer(): pl.pallas_call(functools.partial(layer_kernel, factor), out_shape=(jax.Sh...  118 us
    unnamed x4, local copies, waits for them, and re-layouts  5.31 us

profile of v2, /device:TPU:0, one launch (start us, length us, event | category | flops | bytes accessed | tf_op | source)
XLA Modules:
  0.0 126.2 jit_solution(7557662781326064452)
XLA Ops:
  0.6 1.2 convert_element_type.3.scale_ref
  1.8 1.4 %copy.13 = s32[1,16,6]{2,1,0:T(8,128)} copy(s32[1,16,6]{1,0,2:T(1,128)} %param.15) | data formatting | bytes 768 | tf_op jit(solution)/shard_map/squeeze | solution.py:487
  3.2 117.7 %layer.1 = (bf16[16,128,1024]{2,1,0:T(8,128)(2,1)}, f32[16,1024]{1,0:T(8,128)}) custom-call(s32[1,32]{1,0:T(1,128)} %send_ref.1, f32[8]{0:T(128)} %convert_element_type.3.scale_ref, s32[16,6]{1,0:T(8,128)} %bitcast.11, s32[1,16]{1,0:T(1,128)} %self_ref.1, bf16[8,128,1024]{2,1,0:T(8,128)(2,1)} %bitcast.10, bf16[16,6,128,128]{3,2,1,0:T(8,128)(2,1)} %bitcast.9, ...), custom_call_target="tpu_custom_call" | custom-call | tf_op jit(solution)/shard_map/layer/pallas_call | solution.py:438
  120.9 0.0 copy-start
  120.9 4.7 %copy.16 = bf16[2048,1024]{1,0:T(8,128)(2,1)} copy(bf16[2048,1024]{1,0:T(8,128)(2,1)} %bitcast.7) | data formatting | bytes 8388608
  125.6 0.0 copy-done
  125.6 0.6 copy.17
Async XLA Ops:
  120.9 4.7 %copy-start = (f32[16,1024]{1,0:T(8,128)S(1)}, f32[16,1024]{1,0:T(8,128)}, u32[]{:S(2)}) copy-start(f32[16,1024]{1,0:T(8,128)} %get-tuple-element.9) | copy-start | bytes 196612

commit v3 on v2

v3 whole, which is shorter than its diff:
```python
import functools
import math

import jax
import jax.numpy as jnp
from jax import lax
from jax.experimental import pallas as pl
from jax.experimental.pallas import tpu as pltpu
from jax.sharding import PartitionSpec as P

MOMENTUM = 0.6
MESH = pl.DeviceIdType.MESH
BLOCK = 128
FEATS = 1024
PHASES = 4
WIDE = FEATS // PHASES
PAIRS = 8
LANES = 128
TARGETS = 16
PIECE = (2, 4, 16, WIDE)
PAIR_LAG = 2
HOP_LAG = 4
F32 = jnp.float32
BF16 = jnp.bfloat16


def dom_of(z, y, c):
    return (z * 4 + y) * 2 + c


def columns(f):
    return pl.ds(pl.multiple_of(f * WIDE, WIDE), WIDE)


def layer_kernel(
    factor,
    send_ref, near_ref, self_ref, scale_vmem, own_hbm, edge_hbm, cache_hbm, wself_hbm, wneigh_hbm, cot_hbm,
    out_hbm, grad_ref,
    own, edge, wself, wneigh, cache, cot, outs, base, look, acc, both_t, delta,
    pool, recv, xfer, got0, got1, sum1, got2, scale_ref,
    load_sem, cache_sem, cot_sem, out_sem,
    send_sem, recv_sem, swap_out, swap_in, pass_sem, take_sem, cross_out, cross_in, hop_out, hop_in, last_out, last_in,
):
    dom, x = lax.axis_index("dom"), lax.axis_index("rep")
    z, y, c = dom // 8, lax.rem(dom // 2, 4), lax.rem(dom, 2)
    right, left = lax.rem(x + 1, 4), lax.rem(x + 3, 4)
    other = (dom_of(z, y, 1 - c), x)

    loads = [
        pltpu.make_async_copy(src, dst, load_sem.at[n])
        for n, (src, dst) in enumerate(((own_hbm, own), (wself_hbm, wself), (wneigh_hbm, wneigh), (edge_hbm, edge)))
    ]

    def cache_copy(f):
        s = lax.rem(f, 2)
        return pltpu.make_async_copy(cache_hbm.at[:, :, columns(f)], cache.at[s], cache_sem.at[s])

    def cot_copy(n):
        return pltpu.make_async_copy(cot_hbm.at[:, :, columns(n)], cot.at[n % 2], cot_sem.at[n % 2])

    def out_copy(n):
        return pltpu.make_async_copy(outs.at[n % 2], out_hbm.at[:, :, columns(n)], out_sem.at[n % 2])

    loads[0].start()

    barrier = pltpu.get_barrier_semaphore()

    @pl.loop(1, 16)
    def _(j):
        to = dom_of(lax.rem(z + j // 4, 4), lax.rem(y + lax.rem(j, 4), 4), c)
        pl.semaphore_signal(barrier, inc=1, device_id=(to, x), device_id_type=MESH)

    @pl.loop(0, 12)
    def _(j):
        to = (dom_of(lax.rem(z + j // 3, 4), y, c), lax.rem(x + 1 + lax.rem(j, 3), 4))
        pl.semaphore_signal(barrier, inc=1, device_id=to, device_id_type=MESH)

    pl.semaphore_signal(barrier, inc=1, device_id=other, device_id_type=MESH)

    def offset(i):
        group, dz = lax.rem(x + lax.rem(i, 2), 4), i // 2
        return group, dz, lax.rem(group + 4 - dz, 4)

    def slot_of(group, dz, dc):
        return group * 8 + dz * 2 + dc

    def staged(f, i, w):
        return pool.at[f, i // 4, lax.rem(i, 4), pl.ds(2 * w, 2)]

    def handed(f, i):
        return xfer.at[f, i // 2, pl.ds(2 * lax.rem(i, 2), 2)]

    def target(f, i, w):
        group, dz, _ = offset(i)
        return recv.at[f, slot_of(group, dz, 0)] if w == 0 else handed(f, i)

    def direct(f, i, w):
        _, dz, dy = offset(i)
        return pltpu.make_async_remote_copy(
            src_ref=staged(f, i, w), dst_ref=target(f, i, w),
            send_sem=send_sem.at[f, i, w], recv_sem=recv_sem.at[f, i, w],
            device_id=(dom_of(lax.rem(z + dz, 4), lax.rem(y + dy, 4), c), x), device_id_type=MESH,
        )

    def leaves(i):
        group, dz, _ = offset(i)
        return group * 4 + dz != 0

    def fill(f):
        @pl.loop(0, PAIRS)
        def _(i):
            _, dz, dy = offset(i)
            pieces = []
            for core in (c, 1 - c):
                chosen = send_ref[0, dom_of(lax.rem(z + dz, 4), lax.rem(y + dy, 4), core)]
                gain = scale_ref[chosen] * MOMENTUM
                pieces.append((own[chosen, :, columns(f)].astype(F32) * gain).astype(BF16).reshape(PIECE))

            @pl.when(leaves(i))
            def _():
                for w in range(2):
                    pool[f, i // 4, lax.rem(i, 4), pl.ds(2 * w, 2)] = pieces[w]

            @pl.when(jnp.logical_not(leaves(i)))
            def _():
                recv[f, 0] = pieces[0]
                xfer[f, i // 2, pl.ds(2 * lax.rem(i, 2), 2)] = pieces[1]

    def send(f, i, w):
        @pl.when(leaves(i))
        def _():
            direct(f, i, w).start()

    def arrive(f, i, w):
        @pl.when(leaves(i))
        def _():
            direct(f, i, w).wait_recv()

    def swap(f, i):
        group, dz, _ = offset(i)
        return pltpu.make_async_remote_copy(
            src_ref=handed(f, i), dst_ref=recv.at[f, slot_of(group, dz, 1)],
            send_sem=swap_out.at[f, i], recv_sem=swap_in.at[f, i],
            device_id=other, device_id_type=MESH,
        )

    def onward(f, i, dc):
        group, dz, _ = offset(i)
        slot = slot_of(group, dz, dc)
        return pltpu.make_async_remote_copy(
            src_ref=recv.at[f, slot], dst_ref=recv.at[f, slot],
            send_sem=pass_sem.at[f, i, dc], recv_sem=take_sem.at[f, i, dc],
            device_id=(dom, jnp.where(lax.rem(i, 2) == 0, right, left)), device_id_type=MESH,
        )

    def taken(f, i, dc):
        group = lax.rem(x + 3 - lax.rem(i, 2), 4)
        slot = slot_of(group, i // 2, dc)
        return pltpu.make_async_remote_copy(
            src_ref=recv.at[f, slot], dst_ref=recv.at[f, slot],
            send_sem=pass_sem.at[f, i, dc], recv_sem=take_sem.at[f, i, dc],
            device_id=(dom, right), device_id_type=MESH,
        )

    def after_swap(f, i):
        swap(f, i).wait_recv()
        onward(f, i, 1).start()
        group, dz, _ = offset(i)
        combine(f, group, dz, 1)

    def dequantize(b):
        rows = (own[b].astype(F32) * scale_ref[b]).astype(BF16)
        own[b] = rows
        both_t[b] = rows.T

    def begin(n):
        base[...] = jnp.dot(
            own[...].reshape(FEATS, FEATS), wself[:, columns(n)], preferred_element_type=F32
        ).reshape(8, BLOCK, WIDE)

        @pl.loop(0, TARGETS)
        def _(t):
            acc[t, :, columns(n)] = base[self_ref[0, t]]

    def combine(f, group, dz, dc):
        dy = lax.rem(group + 4 - dz, 4)
        src = dom_of(lax.rem(z + 4 - dz, 4), lax.rem(y + 4 - dy, 4), c if dc == 0 else 1 - c)
        fresh = recv[f, slot_of(group, dz, dc)].reshape(BLOCK, WIDE).astype(F32)
        side = lax.rem(f, 2)
        look[side, 8 + src] = (fresh + (1.0 - MOMENTUM) * cache[side, src].astype(F32)).astype(BF16)

    def combine_taken(f, i):
        for dc in (1, 0):
            taken(f, i, dc).wait_recv()
            combine(f, lax.rem(x + 3 - lax.rem(i, 2), 4), i // 2, dc)

    def aggregate(f, g):
        parts = []
        for q in range(4):
            t = 4 * g + q
            coefs = jnp.concatenate([edge[t, k] for k in range(6)], axis=1)
            rows = jnp.concatenate([look[lax.rem(f, 2), near_ref[k, 0, t]] for k in range(6)], axis=0)
            part = jnp.dot(coefs, rows, preferred_element_type=F32).astype(BF16)
            both_t[8 + t, columns(f), :] = part.T
            parts.append(part)
        whole = jnp.concatenate(parts, axis=0)
        for n in range(PHASES):
            cols = slice(n * WIDE, (n + 1) * WIDE)
            more = jnp.dot(whole, wneigh[columns(f), cols], preferred_element_type=F32)
            acc[pl.ds(4 * g, 4), :, cols] += more.reshape(4, BLOCK, WIDE)

    lane = lax.broadcasted_iota(jnp.int32, (1, 8), 1)
    for b in range(8):
        scale_ref[b] = jnp.sum(jnp.where(lane == b, scale_vmem[...].astype(F32), 0.0))

    loads[0].wait()
    fill(0)
    pl.semaphore_wait(barrier, 28)
    for f in range(PHASES):
        if f:
            fill(f)
        for w in (1, 0):
            @pl.loop(0, PAIRS)
            def _(i):
                send(f, i, w)

        if f == 0:
            for n in range(2):
                cache_copy(n).start()

    for load in loads[1:]:
        load.start()
    for n in range(2):
        cot_copy(n).start()

    @pl.loop(0, PHASES)
    def _(f):
        cache_copy(f).wait()

        @pl.loop(0, PAIRS)
        def _(i):
            arrive(f, i, 1)
            swap(f, i).start()

            @pl.when(i >= 1)
            def _():
                after_swap(f, i - 1)

            @pl.when(f == 0)
            def _():
                dequantize(i)

            @pl.when((f == 1) & (i == 0))
            def _():
                for load in loads[1:]:
                    load.wait()

            @pl.when((f == 1) & (i < PHASES))
            def _():
                begin(i)

            @pl.when(f >= 1)
            def _():
                combine_taken(f - 1, i)

        @pl.loop(0, PAIRS)
        def _(i):
            arrive(f, i, 0)
            onward(f, i, 0).start()

            @pl.when(i == 0)
            def _():
                after_swap(f, PAIRS - 1)

            group, dz, _ = offset(i)
            combine(f, group, dz, 0)
            look[lax.rem(f, 2), i] = own[i, :, columns(f)]

            @pl.when((f >= 1) & (i == 0) & (f + 1 < PHASES))
            def _():
                cache_copy(f + 1).start()

            @pl.when((f >= 1) & (lax.rem(i, 2) == 0))
            def _():
                aggregate(f - 1, i // 2)

    @pl.loop(0, PAIRS)
    def _(i):
        combine_taken(PHASES - 1, i)

    @pl.loop(0, 4)
    def _(g):
        aggregate(PHASES - 1, g)

    @pl.loop(0, PHASES)
    def _(f):
        @pl.loop(0, PAIRS)
        def _(i):
            @pl.when(leaves(i))
            def _():
                for w in range(2):
                    direct(f, i, w).wait_send()

            swap(f, i).wait_send()

    def cross(n, zz):
        return pltpu.make_async_remote_copy(
            src_ref=pool.at[n, 1 - c, zz], dst_ref=got0.at[n, zz],
            send_sem=cross_out.at[n, zz], recv_sem=cross_in.at[n, zz],
            device_id=other, device_id_type=MESH,
        )

    def hop(n, h, zz, off):
        lanes = pl.ds(h * LANES, LANES)
        if h == 0:
            goal = lax.rem(x + off, 4)
            src, to = xfer.at[n, zz, :, goal, :, lanes], (dom, goal)
        else:
            goal = lax.rem(y + off, 4)
            src, to = xfer.at[n, zz, goal, :, :, lanes], (dom_of(z, goal, c), x)
        return pltpu.make_async_remote_copy(
            src_ref=src, dst_ref=got1.at[n, h, off - 1, zz],
            send_sem=hop_out.at[n, h, zz, off - 1], recv_sem=hop_in.at[n, h, zz, off - 1],
            device_id=to, device_id_type=MESH,
        )

    def last(n, h, zz, k, j):
        goal = lax.rem((y if h == 0 else x) + k, 4)
        to = (dom_of(zz, goal, c), x) if h == 0 else (dom_of(zz, y, c), goal)
        return pltpu.make_async_remote_copy(
            src_ref=sum1.at[n, h, zz, goal], dst_ref=got2.at[n, h, j],
            send_sem=last_out.at[n, h, j], recv_sem=last_in.at[n, h, j],
            device_id=to, device_id_type=MESH,
        )

    def pair_up(tile):
        n, zz = tile // 4, lax.rem(tile, 4)
        cross(n, zz).wait_recv()
        xfer[n, zz] = (pool[n, c, zz].astype(F32) + got0[n, zz].astype(F32)).astype(BF16)
        for off in (2, 1, 3):
            for h in range(2):
                hop(n, h, zz, off).start()

    def spread(tile):
        n, zz = tile // 4, lax.rem(tile, 4)
        for h in range(2):
            for off in (1, 2, 3):
                hop(n, h, zz, off).wait_recv()
            mine = (xfer[n, zz, :, x] if h == 0 else xfer[n, zz, y])[:, :, h * LANES:(h + 1) * LANES].astype(F32)
            for off in range(3):
                mine = mine + got1[n, h, off, zz].astype(F32)
            sum1[n, h, zz] = mine.astype(BF16)
        dz = lax.rem(zz + 4 - z, 4)
        for k in (2, 1, 3):
            for h in range(2):
                last(n, h, zz, k, dz * 4 + k).start()

        @pl.when(dz != 0)
        def _():
            for h in range(2):
                last(n, h, zz, 0, dz * 4).start()

    def close(n):
        for h in range(2):
            @pl.loop(1, 16)
            def _(j):
                last(n, h, lax.rem(z + j // 4, 4), lax.rem(j, 4), j).wait_recv()

            part = sum1[n, h, z, y if h == 0 else x].astype(F32)
            for j in range(1, 16):
                part = part + got2[n, h, j].astype(F32)
            grad_ref[:, (2 * n + h) * LANES:(2 * n + h + 1) * LANES] = part * factor

    def activate(n, t):
        pre = acc[t, :, n * WIDE:(n + 1) * WIDE]
        gate = jax.nn.sigmoid(pre)
        outs[n % 2, t] = (pre * gate).astype(BF16)
        delta[n % 2, t] = (cot[n % 2, t].astype(F32) * gate * (1.0 + pre * (1.0 - gate))).astype(BF16)

    def before(n):
        cot_copy(n).wait()
        if n >= 2:
            out_copy(n - 2).wait()

    def after(n):
        out_copy(n).start()
        if n + 2 < PHASES:
            cot_copy(n + 2).start()

    before(0)

    @pl.loop(0, TARGETS)
    def _(t):
        activate(0, t)

    after(0)

    for n in range(PHASES):
        if n + 1 < PHASES:
            before(n + 1)

        @pl.loop(0, 4)
        def _(zz):
            rows = pl.ds(pl.multiple_of(lax.rem(zz, 2) * 512, 512), 512)
            lhs = [both_t[jnp.where(zz < 2, self_ref[0, t], 8 + t), rows, :] for t in range(TARGETS)]
            part = jnp.dot(
                jnp.concatenate(lhs, axis=1), delta[n % 2].reshape(TARGETS * BLOCK, WIDE),
                preferred_element_type=F32,
            ).astype(BF16).reshape(4, 2, 4, 16, WIDE)
            for core in range(2):
                pool[n, core, zz] = part[:, core]
            cross(n, zz).start()
            if n + 1 < PHASES:
                for q in range(4):
                    activate(n + 1, 4 * zz + q)

            tile = 4 * n + zz

            @pl.when(tile >= PAIR_LAG)
            def _():
                pair_up(tile - PAIR_LAG)

            @pl.when(tile >= PAIR_LAG + HOP_LAG)
            def _():
                spread(tile - PAIR_LAG - HOP_LAG)

        if n + 1 < PHASES:
            after(n + 1)

    tiles = 4 * PHASES
    for tile in range(tiles - PAIR_LAG, tiles):
        pair_up(jnp.int32(tile))

    @pl.loop(tiles - PAIR_LAG - HOP_LAG, tiles)
    def _(tile):
        spread(tile)

    for n in range(PHASES):
        close(n)

    out_copy(PHASES - 2).wait()
    out_copy(PHASES - 1).wait()

    @pl.loop(0, PHASES)
    def _(f):
        @pl.loop(0, PAIRS)
        def _(i):
            for dc in range(2):
                onward(f, i, dc).wait_send()

        @pl.loop(0, 4)
        def _(zz):
            cross(f, zz).wait_send()
            for h in range(2):
                for off in (1, 2, 3):
                    hop(f, h, zz, off).wait_send()

        for h in range(2):
            @pl.loop(1, 16)
            def _(j):
                last(f, h, lax.rem(z + j // 4, 4), lax.rem(j, 4), j).wait_send()


def layer(factor, send_list, near, batch, scale, own, edges, cache, w_self, w_neigh, cot):
    vmem = pl.BlockSpec(memory_space=pltpu.VMEM)
    smem = pl.BlockSpec(memory_space=pltpu.SMEM)
    hbm = pl.BlockSpec(memory_space=pl.ANY)
    dma = pltpu.SemaphoreType.DMA
    return pl.pallas_call(
        functools.partial(layer_kernel, factor),
        out_shape=(
            jax.ShapeDtypeStruct((TARGETS, BLOCK, FEATS), BF16),
            jax.ShapeDtypeStruct((16, FEATS), F32),
        ),
        in_specs=[smem] * 3 + [vmem] + [hbm] * 6,
        out_specs=(hbm, vmem),
        scratch_shapes=[
            pltpu.VMEM((8, BLOCK, FEATS), BF16),
            pltpu.VMEM((TARGETS, 6, BLOCK, BLOCK), BF16),
            pltpu.VMEM((FEATS, FEATS), BF16),
            pltpu.VMEM((FEATS, FEATS), BF16),
            pltpu.VMEM((2, 32, BLOCK, WIDE), BF16),
            pltpu.VMEM((2, TARGETS, BLOCK, WIDE), BF16),
            pltpu.VMEM((2, TARGETS, BLOCK, WIDE), BF16),
            pltpu.VMEM((8, BLOCK, WIDE), F32),
            pltpu.VMEM((2, 40, BLOCK, WIDE), BF16),
            pltpu.VMEM((TARGETS, BLOCK, FEATS), F32),
            pltpu.VMEM((8 + TARGETS, FEATS, BLOCK), BF16),
            pltpu.VMEM((2, TARGETS, BLOCK, WIDE), BF16),
            pltpu.VMEM((PHASES, 2, 4, 4, 4, 16, WIDE), BF16),
            pltpu.VMEM((PHASES, 32) + PIECE, BF16),
            pltpu.VMEM((PHASES, 4, 4, 4, 16, WIDE), BF16),
            pltpu.VMEM((PHASES, 4, 4, 4, 16, WIDE), BF16),
            pltpu.VMEM((PHASES, 2, 3, 4, 4, 16, LANES), BF16),
            pltpu.VMEM((PHASES, 2, 4, 4, 16, LANES), BF16),
            pltpu.VMEM((PHASES, 2, 16, 16, LANES), BF16),
            pltpu.SMEM((8,), F32),
            dma((4,)), dma((2,)), dma((2,)), dma((2,)),
            dma((PHASES, PAIRS, 2)), dma((PHASES, PAIRS, 2)), dma((PHASES, PAIRS)), dma((PHASES, PAIRS)),
            dma((PHASES, PAIRS, 2)), dma((PHASES, PAIRS, 2)), dma((PHASES, 4)), dma((PHASES, 4)),
            dma((PHASES, 2, 4, 3)), dma((PHASES, 2, 4, 3)), dma((PHASES, 2, 16)), dma((PHASES, 2, 16)),
        ],
        compiler_params=pltpu.CompilerParams(
            collective_id=0, has_side_effects=True, vmem_limit_bytes=62 * 2**20
        ),
        name="layer",
    )(send_list, near, batch, scale, own, edges, cache, w_self, w_neigh, cot)


def on_device(
    own_values, own_scale, halo_cache, send_list, batch_ids, neighbor_blocks, edge_tiles, w_self, w_neigh, cotangent,
):
    rows = cotangent.shape[0] * lax.axis_size("dom") * lax.axis_size("rep")
    output_rows, grads = layer(
        1.0 / math.sqrt(rows), send_list, neighbor_blocks.transpose(2, 0, 1), batch_ids, own_scale.reshape(1, 8),
        own_values.reshape(8, BLOCK, FEATS), edge_tiles[0], halo_cache.reshape(32, BLOCK, FEATS),
        w_self, w_neigh, cotangent.reshape(TARGETS, BLOCK, FEATS),
    )
    return output_rows.reshape(-1, FEATS), grads


def solution(mesh):
    placed = (
        P("dom", None), P("dom"), P("dom", None), P("dom", None), P("dom", "rep"), P("dom", "rep", None),
        P("dom", "rep", None, None, None), P(), P(), P(("dom", "rep"), None),
    )
    return jax.shard_map(
        on_device,
        mesh=mesh,
        in_specs=placed,
        out_specs=(P(("dom", "rep"), None), P(("dom", "rep"), None)),
        check_vma=False,
    )
```

time: 126 us -> 111 us (0.88)
  Pallas kernels: 118 us -> 105 us
  local copies, waits for them, and re-layouts: 6.66 us -> 5.31 us
    pallas_call x1, Pallas kernels: 118 us -> 105 us  [layer(): pl.pallas_call(functools.partial(layer_kernel, factor), out_shape=(jax.Sh...]
    squeeze x1 -> x0, local copies, waits for them, and re-layouts: 1.36 us -> none  [on_device(): neighbor_blocks[0]]
where the time goes in v3:
time: 111 us
  Pallas kernels  105 us (95%)
  local copies, waits for them, and re-layouts  5.31 us (5%)
    pallas_call x1, Pallas kernels, layer(): pl.pallas_call(functools.partial(layer_kernel, factor), out_shape=(jax.Sh...  105 us
    unnamed x4, local copies, waits for them, and re-layouts  5.31 us

profile of v3, /device:TPU:0, one launch (start us, length us, event | category | flops | bytes accessed | tf_op | source)
XLA Modules:
  0.0 111.1 jit_solution(15738192827045325473)
XLA Ops:
  0.6 105.2 %layer.1 = (bf16[16,128,1024]{2,1,0:T(8,128)(2,1)}, f32[16,1024]{1,0:T(8,128)}) custom-call(s32[1,32]{1,0:T(1,128)} %send_ref.1, s32[6,1,16]{2,1,0:T(1,128)} %bitcast.12, s32[1,16]{1,0:T(1,128)} %self_ref.1, bf16[1,8]{1,0:T(2,128)(2,1)} %bitcast.13, bf16[8,128,1024]{2,1,0:T(8,128)(2,1)} %bitcast.11, bf16[16,6,128,128]{3,2,1,0:T(8,128)(2,1)} %bitcast.10, ...), custom_call_target="tpu_custom_call" | custom-call | tf_op jit(solution)/shard_map/layer/pallas_call | solution.py:469
  105.8 0.0 copy-start
  105.8 4.7 %copy.14 = bf16[2048,1024]{1,0:T(8,128)(2,1)} copy(bf16[2048,1024]{1,0:T(8,128)(2,1)} %bitcast.8) | data formatting | bytes 8388608
  110.5 0.0 copy-done
  110.5 0.6 copy.15
Async XLA Ops:
  105.8 4.7 %copy-start = (f32[16,1024]{1,0:T(8,128)S(1)}, f32[16,1024]{1,0:T(8,128)}, u32[]{:S(2)}) copy-start(f32[16,1024]{1,0:T(8,128)} %get-tuple-element.9) | copy-start | bytes 196612

commit v4 on v3

v4 whole, which is shorter than its diff:
```python
import functools
import math

import jax
import jax.numpy as jnp
from jax import lax
from jax.experimental import pallas as pl
from jax.experimental.pallas import tpu as pltpu
from jax.sharding import PartitionSpec as P

MOMENTUM = 0.6
MESH = pl.DeviceIdType.MESH
BLOCK = 128
FEATS = 1024
PHASES = 4
WIDE = FEATS // PHASES
PAIRS = 8
TARGETS = 16
PIECE = (2, 4, 16, WIDE)
SWAP_LAG = 2
F32 = jnp.float32
BF16 = jnp.bfloat16


def dom_of(z, y, c):
    return (z * 4 + y) * 2 + c


def columns(f):
    return pl.ds(pl.multiple_of(f * WIDE, WIDE), WIDE)


def layer_kernel(
    factor,
    send_ref, near_ref, self_ref, scale_vmem, own_hbm, edge_hbm, cache_hbm, wself_hbm, wneigh_hbm, cot_hbm,
    out_ref, grad_ref,
    own, edge, wneigh, cache, cot, base, look, acc, both_t, delta,
    pool, recv, xfer, got0, got1, sum1, got2, scale_ref,
    load_sem, wself_sem, cache_sem, cot_sem,
    send_sem, recv_sem, swap_out, swap_in, pass_sem, take_sem, cross_out, cross_in, hop_out, hop_in, last_out, last_in,
):
    dom, x = lax.axis_index("dom"), lax.axis_index("rep")
    z, y, c = dom // 8, lax.rem(dom // 2, 4), lax.rem(dom, 2)
    right, left = lax.rem(x + 1, 4), lax.rem(x + 3, 4)
    other = (dom_of(z, y, 1 - c), x)

    loads = [
        pltpu.make_async_copy(src, dst, load_sem.at[n])
        for n, (src, dst) in enumerate(((own_hbm, own), (wneigh_hbm, wneigh), (edge_hbm, edge)))
    ]

    def wself(n):
        return delta.at[n // 2, pl.ds(lax.rem(n, 2) * 8, 8)]

    def wself_copy(n):
        return pltpu.make_async_copy(wself_hbm.at[:, :, columns(n)], wself(n), wself_sem.at[n])

    def cache_copy(f):
        s = lax.rem(f, 2)
        return pltpu.make_async_copy(cache_hbm.at[:, :, columns(f)], cache.at[s], cache_sem.at[s])

    def cot_copy(n):
        return pltpu.make_async_copy(cot_hbm.at[:, :, columns(n)], cot.at[n % 2], cot_sem.at[n % 2])

    loads[0].start()

    barrier = pltpu.get_barrier_semaphore()

    @pl.loop(1, 16)
    def _(j):
        to = dom_of(lax.rem(z + j // 4, 4), lax.rem(y + lax.rem(j, 4), 4), c)
        pl.semaphore_signal(barrier, inc=1, device_id=(to, x), device_id_type=MESH)

    @pl.loop(0, 12)
    def _(j):
        to = (dom_of(lax.rem(z + j // 3, 4), y, c), lax.rem(x + 1 + lax.rem(j, 3), 4))
        pl.semaphore_signal(barrier, inc=1, device_id=to, device_id_type=MESH)

    pl.semaphore_signal(barrier, inc=1, device_id=other, device_id_type=MESH)

    def offset(i):
        group, dz = lax.rem(x + lax.rem(i, 2), 4), i // 2
        return group, dz, lax.rem(group + 4 - dz, 4)

    def slot_of(group, dz, dc):
        return group * 8 + dz * 2 + dc

    def staged(f, i, w):
        return pool.at[f, i // 4, lax.rem(i, 4), pl.ds(2 * w, 2)]

    def handed(f, i):
        return xfer.at[f, i // 2, pl.ds(2 * lax.rem(i, 2), 2)]

    def target(f, i, w):
        group, dz, _ = offset(i)
        return recv.at[f, slot_of(group, dz, 0)] if w == 0 else handed(f, i)

    def direct(f, i, w):
        _, dz, dy = offset(i)
        return pltpu.make_async_remote_copy(
            src_ref=staged(f, i, w), dst_ref=target(f, i, w),
            send_sem=send_sem.at[i], recv_sem=recv_sem.at[f, i, w],
            device_id=(dom_of(lax.rem(z + dz, 4), lax.rem(y + dy, 4), c), x), device_id_type=MESH,
        )

    def leaves(i):
        group, dz, _ = offset(i)
        return group * 4 + dz != 0

    def fill(f):
        @pl.loop(0, PAIRS)
        def _(i):
            _, dz, dy = offset(i)
            pieces = []
            for core in (c, 1 - c):
                chosen = send_ref[0, dom_of(lax.rem(z + dz, 4), lax.rem(y + dy, 4), core)]
                gain = scale_ref[chosen] * MOMENTUM
                pieces.append((own[chosen, :, columns(f)].astype(F32) * gain).astype(BF16).reshape(PIECE))

            @pl.when(leaves(i))
            def _():
                for w in range(2):
                    pool[f, i // 4, lax.rem(i, 4), pl.ds(2 * w, 2)] = pieces[w]

            @pl.when(jnp.logical_not(leaves(i)))
            def _():
                recv[f, 0] = pieces[0]
                xfer[f, i // 2, pl.ds(2 * lax.rem(i, 2), 2)] = pieces[1]

    def send(f, i, w):
        @pl.when(leaves(i))
        def _():
            direct(f, i, w).start()

    def arrive(f, i, w):
        @pl.when(leaves(i))
        def _():
            direct(f, i, w).wait_recv()

    def swap(f, i):
        group, dz, _ = offset(i)
        return pltpu.make_async_remote_copy(
            src_ref=handed(f, i), dst_ref=recv.at[f, slot_of(group, dz, 1)],
            send_sem=swap_out, recv_sem=swap_in.at[f, i],
            device_id=other, device_id_type=MESH,
        )

    def onward(f, i, dc):
        group, dz, _ = offset(i)
        slot = slot_of(group, dz, dc)
        return pltpu.make_async_remote_copy(
            src_ref=recv.at[f, slot], dst_ref=recv.at[f, slot],
            send_sem=pass_sem, recv_sem=take_sem.at[f, i],
            device_id=(dom, jnp.where(lax.rem(i, 2) == 0, right, left)), device_id_type=MESH,
        )

    def taken(f, i):
        both = recv.at[f, pl.ds(slot_of(lax.rem(x + 3 - lax.rem(i, 2), 4), i // 2, 0), 2)]
        return pltpu.make_async_copy(both, both, take_sem.at[f, i])

    def after_swap(f, i):
        swap(f, i).wait_recv()
        onward(f, i, 1).start()
        group, dz, _ = offset(i)
        combine(f, group, dz, 1)

    def dequantize(b):
        rows = (own[b].astype(F32) * scale_ref[b]).astype(BF16)
        own[b] = rows
        both_t[b] = rows.T

    def begin(n):
        wself_copy(n).wait()
        base[...] = jnp.dot(
            own[...].reshape(FEATS, FEATS), wself(n)[...].reshape(FEATS, WIDE), preferred_element_type=F32
        ).reshape(8, BLOCK, WIDE)

        @pl.loop(0, TARGETS)
        def _(t):
            acc[t, :, columns(n)] = base[self_ref[0, t]]

    def combine(f, group, dz, dc):
        dy = lax.rem(group + 4 - dz, 4)
        src = dom_of(lax.rem(z + 4 - dz, 4), lax.rem(y + 4 - dy, 4), c if dc == 0 else 1 - c)
        fresh = recv[f, slot_of(group, dz, dc)].reshape(BLOCK, WIDE).astype(F32)
        side = lax.rem(f, 2)
        look[side, 8 + src] = (fresh + (1.0 - MOMENTUM) * cache[side, src].astype(F32)).astype(BF16)

    def combine_taken(f, i):
        taken(f, i).wait()
        for dc in range(2):
            combine(f, lax.rem(x + 3 - lax.rem(i, 2), 4), i // 2, dc)

    def aggregate(f, g):
        parts = []
        for q in range(4):
            t = 4 * g + q
            coefs = jnp.concatenate([edge[t, k] for k in range(6)], axis=1)
            rows = jnp.concatenate([look[lax.rem(f, 2), near_ref[k, 0, t]] for k in range(6)], axis=0)
            part = jnp.dot(coefs, rows, preferred_element_type=F32).astype(BF16)
            both_t[8 + t, columns(f), :] = part.T
            parts.append(part)
        whole = jnp.concatenate(parts, axis=0)
        for n in range(PHASES):
            cols = slice(n * WIDE, (n + 1) * WIDE)
            more = jnp.dot(whole, wneigh[columns(f), cols], preferred_element_type=F32)
            acc[pl.ds(4 * g, 4), :, cols] += more.reshape(4, BLOCK, WIDE)

    lane = lax.broadcasted_iota(jnp.int32, (1, 8), 1)
    for b in range(8):
        scale_ref[b] = jnp.sum(jnp.where(lane == b, scale_vmem[...].astype(F32), 0.0))

    loads[0].wait()
    fill(0)
    pl.semaphore_wait(barrier, 28)
    for f in range(PHASES):
        if f:
            fill(f)
        for w in (1, 0):
            @pl.loop(0, PAIRS)
            def _(i):
                send(f, i, w)

        if f == 0:
            for n in range(2):
                cache_copy(n).start()

    for n in range(PHASES):
        wself_copy(n).start()
    for load in loads[1:]:
        load.start()
    for n in range(2):
        cot_copy(n).start()

    @pl.loop(0, PHASES)
    def _(f):
        cache_copy(f).wait()

        @pl.loop(0, PAIRS)
        def _(i):
            arrive(f, i, 1)
            swap(f, i).start()

            @pl.when(i >= SWAP_LAG)
            def _():
                after_swap(f, i - SWAP_LAG)

            @pl.when(f == 0)
            def _():
                dequantize(i)

            @pl.when((f == 1) & (i == 0))
            def _():
                for load in loads[1:]:
                    load.wait()

            @pl.when((f == 1) & (i < PHASES))
            def _():
                begin(i)

            @pl.when((f >= 1) & (i >= 4))
            def _():
                combine_taken(f - 1, i - 4)

        @pl.loop(0, PAIRS)
        def _(i):
            arrive(f, i, 0)
            onward(f, i, 0).start()

            @pl.when(i < SWAP_LAG)
            def _():
                after_swap(f, i + PAIRS - SWAP_LAG)

            group, dz, _ = offset(i)
            combine(f, group, dz, 0)
            look[lax.rem(f, 2), i] = own[i, :, columns(f)]

            @pl.when((f >= 1) & (i < 4))
            def _():
                combine_taken(f - 1, i + 4)

            @pl.when((f >= 1) & (i == 4) & (f + 1 < PHASES))
            def _():
                cache_copy(f + 1).start()

            @pl.when((f >= 1) & (i >= 4))
            def _():
                aggregate(f - 1, i - 4)

    @pl.loop(0, PAIRS)
    def _(i):
        combine_taken(PHASES - 1, i)

    for g in range(4):
        aggregate(PHASES - 1, g)

    @pl.loop(0, PAIRS)
    def _(i):
        @pl.when(leaves(i))
        def _():
            pltpu.make_async_copy(xfer.at[0], xfer.at[0], send_sem.at[i]).wait()

    pltpu.make_async_copy(xfer, xfer, swap_out).wait()

    def cross(n):
        return pltpu.make_async_remote_copy(
            src_ref=pool.at[n, 1 - c], dst_ref=got0.at[n],
            send_sem=cross_out, recv_sem=cross_in.at[n],
            device_id=other, device_id_type=MESH,
        )

    def hop(n, h, off):
        if h == 0:
            goal = lax.rem(x + off, 4)
            src, to = xfer.at[n, pl.ds(0, 2), :, goal], (dom, goal)
        else:
            goal = lax.rem(y + off, 4)
            src, to = xfer.at[n, pl.ds(2, 2), goal], (dom_of(z, goal, c), x)
        return pltpu.make_async_remote_copy(
            src_ref=src, dst_ref=got1.at[n, h, off - 1],
            send_sem=hop_out, recv_sem=hop_in.at[n],
            device_id=to, device_id_type=MESH,
        )

    def last(n, zz, k):
        goal = lax.rem((y if zz < 2 else x) + k, 4)
        return pltpu.make_async_remote_copy(
            src_ref=sum1.at[n, zz, goal], dst_ref=got2.at[n, lax.rem(zz + 4 - z, 4) * 4 + k],
            send_sem=last_out, recv_sem=last_in.at[n],
            device_id=(dom_of(zz, goal, c), x) if zz < 2 else (dom_of(zz, y, c), goal), device_id_type=MESH,
        )

    def pair_up(n):
        cross(n).wait_recv()
        for zz in range(4):
            xfer[n, zz] = (pool[n, c, zz].astype(F32) + got0[n, zz].astype(F32)).astype(BF16)
        for off in (2, 1, 3):
            for h in range(2):
                hop(n, h, off).start()

    def spread(n):
        pltpu.make_async_copy(got1.at[n], got1.at[n], hop_in.at[n]).wait()
        for h in range(2):
            part = (xfer[n, 0:2, :, x] if h == 0 else xfer[n, 2:4, y]).astype(F32)
            for off in range(3):
                part = part + got1[n, h, off].astype(F32)
            sum1[n, 2 * h:2 * h + 2] = part.astype(BF16)
        for k in (2, 1, 3, 0):
            for zz in range(4):
                if k:
                    last(n, zz, k).start()
                else:
                    pl.when(zz != z)(last(n, zz, k).start)

    def close(n):
        came = got2.at[n, pl.ds(1, 15)]
        pltpu.make_async_copy(came, came, last_in.at[n]).wait()
        part = sum1[n, z, jnp.where(z < 2, y, x)].astype(F32)
        for j in range(1, 16):
            part = part + got2[n, j].astype(F32)
        grad_ref[:, n * WIDE:(n + 1) * WIDE] = part * factor

    def activate(n, t):
        pre = acc[t, :, n * WIDE:(n + 1) * WIDE]
        gate = jax.nn.sigmoid(pre)
        out_ref[t, :, n * WIDE:(n + 1) * WIDE] = (pre * gate).astype(BF16)
        delta[n % 2, t] = (cot[n % 2, t].astype(F32) * gate * (1.0 + pre * (1.0 - gate))).astype(BF16)

    def before(n):
        cot_copy(n).wait()

    def after(n):
        if n + 2 < PHASES:
            cot_copy(n + 2).start()

    before(0)

    @pl.loop(0, TARGETS // 4)
    def _(g):
        for q in range(4):
            activate(0, 4 * g + q)

    after(0)
    for n in range(PHASES):
        if n + 1 < PHASES:
            before(n + 1)

        @pl.loop(0, 2)
        def _(half):
            lhs = [both_t[jnp.where(half == 0, self_ref[0, t], 8 + t)] for t in range(TARGETS)]
            part = jnp.dot(
                jnp.concatenate(lhs, axis=1), delta[n % 2].reshape(TARGETS * BLOCK, WIDE), preferred_element_type=F32
            ).astype(BF16).reshape(2, 4, 2, 4, 16, WIDE)
            for core in range(2):
                pool[n, core, pl.ds(2 * half, 2)] = part[:, :, core]
            if n + 1 < PHASES:
                for q in range(8):
                    activate(n + 1, 8 * half + q)

        cross(n).start()
        if n + 1 < PHASES:
            after(n + 1)
        if n >= 1:
            pair_up(n - 1)
        if n >= 2:
            spread(n - 2)

    pair_up(PHASES - 1)
    spread(PHASES - 2)
    for n in range(PHASES - 2):
        close(n)
    spread(PHASES - 1)
    close(PHASES - 2)
    close(PHASES - 1)

    pltpu.make_async_copy(pool, pool, pass_sem).wait()
    pltpu.make_async_copy(got0, got0, cross_out).wait()
    pltpu.make_async_copy(got1, got1, hop_out).wait()
    went = got2.at[:, pl.ds(1, 15)]
    pltpu.make_async_copy(went, went, last_out).wait()


def layer(factor, send_list, near, batch, scale, own, edges, cache, w_self, w_neigh, cot):
    vmem = pl.BlockSpec(memory_space=pltpu.VMEM)
    smem = pl.BlockSpec(memory_space=pltpu.SMEM)
    hbm = pl.BlockSpec(memory_space=pl.ANY)
    dma = pltpu.SemaphoreType.DMA
    return pl.pallas_call(
        functools.partial(layer_kernel, factor),
        out_shape=(
            pltpu.VMEM((TARGETS, BLOCK, FEATS), BF16),
            pltpu.VMEM((16, FEATS), F32),
        ),
        in_specs=[smem] * 3 + [vmem] + [hbm] * 6,
        out_specs=(vmem, vmem),
        scratch_shapes=[
            pltpu.VMEM((8, BLOCK, FEATS), BF16),
            pltpu.VMEM((TARGETS, 6, BLOCK, BLOCK), BF16),
            pltpu.VMEM((FEATS, FEATS), BF16),
            pltpu.VMEM((2, 32, BLOCK, WIDE), BF16),
            pltpu.VMEM((2, TARGETS, BLOCK, WIDE), BF16),
            pltpu.VMEM((8, BLOCK, WIDE), F32),
            pltpu.VMEM((2, 40, BLOCK, WIDE), BF16),
            pltpu.VMEM((TARGETS, BLOCK, FEATS), F32),
            pltpu.VMEM((8 + TARGETS, FEATS, BLOCK), BF16),
            pltpu.VMEM((2, TARGETS, BLOCK, WIDE), BF16),
            pltpu.VMEM((PHASES, 2, 4, 4, 4, 16, WIDE), BF16),
            pltpu.VMEM((PHASES, 32) + PIECE, BF16),
            pltpu.VMEM((PHASES, 4, 4, 4, 16, WIDE), BF16),
            pltpu.VMEM((PHASES, 4, 4, 4, 16, WIDE), BF16),
            pltpu.VMEM((PHASES, 2, 3, 2, 4, 16, WIDE), BF16),
            pltpu.VMEM((PHASES, 4, 4, 16, WIDE), BF16),
            pltpu.VMEM((PHASES, 16, 16, WIDE), BF16),
            pltpu.SMEM((8,), F32),
            dma((3,)), dma((PHASES,)), dma((2,)), dma((2,)),
            dma((PAIRS,)), dma((PHASES, PAIRS, 2)), dma, dma((PHASES, PAIRS)), dma, dma((PHASES, PAIRS)),
            dma, dma((PHASES,)), dma, dma((PHASES,)), dma, dma((PHASES,)),
        ],
        compiler_params=pltpu.CompilerParams(
            collective_id=0, has_side_effects=True, vmem_limit_bytes=58 * 2**20
        ),
        name="layer",
    )(send_list, near, batch, scale, own, edges, cache, w_self, w_neigh, cot)


def on_device(
    own_values, own_scale, halo_cache, send_list, batch_ids, neighbor_blocks, edge_tiles, w_self, w_neigh, cotangent,
):
    rows = cotangent.shape[0] * lax.axis_size("dom") * lax.axis_size("rep")
    output_rows, grads = layer(
        1.0 / math.sqrt(rows), send_list, neighbor_blocks.transpose(2, 0, 1), batch_ids, own_scale.reshape(1, 8),
        own_values.reshape(8, BLOCK, FEATS), edge_tiles[0], halo_cache.reshape(32, BLOCK, FEATS),
        w_self.reshape(8, BLOCK, FEATS), w_neigh, cotangent.reshape(TARGETS, BLOCK, FEATS),
    )
    return output_rows.reshape(-1, FEATS), grads


def solution(mesh):
    placed = (
        P("dom", None), P("dom"), P("dom", None), P("dom", None), P("dom", "rep"), P("dom", "rep", None),
        P("dom", "rep", None, None, None), P(), P(), P(("dom", "rep"), None),
    )
    return jax.shard_map(
        on_device,
        mesh=mesh,
        in_specs=placed,
        out_specs=(P(("dom", "rep"), None), P(("dom", "rep"), None)),
        check_vma=False,
    )
```

time: 111 us -> 102 us (0.919)
  Pallas kernels: 105 us -> 98.8 us
  local copies, waits for them, and re-layouts: 5.31 us -> 2.64 us
    pallas_call x1, Pallas kernels: 105 us -> 98.8 us  [layer(): pl.pallas_call(functools.partial(layer_kernel, factor), out_shape=(pltpu....]
    unnamed x4 -> x2, local copies, waits for them, and re-layouts: 5.31 us -> 2.64 us
where the time goes in v4:
time: 102 us
  Pallas kernels  98.8 us (97%)
  local copies, waits for them, and re-layouts  2.64 us (3%)
    pallas_call x1, Pallas kernels, layer(): pl.pallas_call(functools.partial(layer_kernel, factor), out_shape=(pltpu....  98.8 us
    unnamed x2, local copies, waits for them, and re-layouts  2.64 us

profile of v4, /device:TPU:0, one launch (start us, length us, event | category | flops | bytes accessed | tf_op | source)
XLA Modules:
  0.0 102.1 jit_solution(13374018461583350412)
XLA Ops:
  0.6 98.8 %layer.1 = (bf16[16,128,1024]{2,1,0:T(8,128)(2,1)S(1)}, f32[16,1024]{1,0:T(8,128)S(1)}) custom-call(s32[1,32]{1,0:T(1,128)} %send_ref.1, s32[6,1,16]{2,1,0:T(1,128)} %bitcast.14, s32[1,16]{1,0:T(1,128)} %self_ref.1, bf16[1,8]{1,0:T(2,128)(2,1)} %bitcast.15, bf16[8,128,1024]{2,1,0:T(8,128)(2,1)} %bitcast.12, bf16[16,6,128,128]{3,2,1,0:T(8,128)(2,1)} %bitcast.11, ...), custom_call_target="tpu_custom_call" | custom-call | tf_op jit(solution)/shard_map/layer/pallas_call | solution.py:428
  99.4 2.0 %copy.14 = bf16[2048,1024]{1,0:T(8,128)(2,1)} copy(bf16[2048,1024]{1,0:T(8,128)(2,1)S(1)} %bitcast.8) | data formatting | bytes 8388608
  101.4 0.6 copy.15

commit v5 on v4

--- a/solution.py
+++ b/solution.py
@@ -17,7 +17,7 @@
 PAIRS = 8
 TARGETS = 16
 PIECE = (2, 4, 16, WIDE)
-SWAP_LAG = 2
+SWAP_LAG = 1
 F32 = jnp.float32
 BF16 = jnp.bfloat16
 
@@ -291,8 +291,24 @@
     def _(i):
         combine_taken(PHASES - 1, i)
 
+    def activate(n, t):
+        pre = acc[t, :, n * WIDE:(n + 1) * WIDE]
+        gate = jax.nn.sigmoid(pre)
+        out_ref[t, :, n * WIDE:(n + 1) * WIDE] = (pre * gate).astype(BF16)
+        delta[n % 2, t] = (cot[n % 2, t].astype(F32) * gate * (1.0 + pre * (1.0 - gate))).astype(BF16)
+
+    def before(n):
+        cot_copy(n).wait()
+
+    def after(n):
+        if n + 2 < PHASES:
+            cot_copy(n + 2).start()
+
+    before(0)
     for g in range(4):
         aggregate(PHASES - 1, g)
+        for q in range(4):
+            activate(0, 4 * g + q)
 
     @pl.loop(0, PAIRS)
     def _(i):
@@ -359,26 +375,6 @@
         for j in range(1, 16):
             part = part + got2[n, j].astype(F32)
         grad_ref[:, n * WIDE:(n + 1) * WIDE] = part * factor
-
-    def activate(n, t):
-        pre = acc[t, :, n * WIDE:(n + 1) * WIDE]
-        gate = jax.nn.sigmoid(pre)
-        out_ref[t, :, n * WIDE:(n + 1) * WIDE] = (pre * gate).astype(BF16)
-        delta[n % 2, t] = (cot[n % 2, t].astype(F32) * gate * (1.0 + pre * (1.0 - gate))).astype(BF16)
-
-    def before(n):
-        cot_copy(n).wait()
-
-    def after(n):
-        if n + 2 < PHASES:
-            cot_copy(n + 2).start()
-
-    before(0)
-
-    @pl.loop(0, TARGETS // 4)
-    def _(g):
-        for q in range(4):
-            activate(0, 4 * g + q)
 
     after(0)
     for n in range(PHASES):

time: 102 us -> 102 us (level)
  no operation moved by 1% of the time
where the time goes in v5:
time: 102 us; the launch traced here: 101 us
  Pallas kernels  98.2 us (96%)
  local copies, waits for them, and re-layouts  2.64 us (3%)
    pallas_call x1, Pallas kernels, layer(): pl.pallas_call(functools.partial(layer_kernel, factor), out_shape=(pltpu....  98.2 us
    unnamed x2, local copies, waits for them, and re-layouts  2.64 us

profile of v5, /device:TPU:0, one launch (start us, length us, event | category | flops | bytes accessed | tf_op | source)
XLA Modules:
  0.0 101.5 jit_solution(11668861724631903461)
XLA Ops:
  0.6 98.2 %layer.1 = (bf16[16,128,1024]{2,1,0:T(8,128)(2,1)S(1)}, f32[16,1024]{1,0:T(8,128)S(1)}) custom-call(s32[1,32]{1,0:T(1,128)} %send_ref.1, s32[6,1,16]{2,1,0:T(1,128)} %bitcast.14, s32[1,16]{1,0:T(1,128)} %self_ref.1, bf16[1,8]{1,0:T(2,128)(2,1)} %bitcast.15, bf16[8,128,1024]{2,1,0:T(8,128)(2,1)} %bitcast.12, bf16[16,6,128,128]{3,2,1,0:T(8,128)(2,1)} %bitcast.11, ...), custom_call_target="tpu_custom_call" | custom-call | tf_op jit(solution)/shard_map/layer/pallas_call | solution.py:424
  98.8 2.0 %copy.14 = bf16[2048,1024]{1,0:T(8,128)(2,1)} copy(bf16[2048,1024]{1,0:T(8,128)(2,1)S(1)} %bitcast.8) | data formatting | bytes 8388608
  100.8 0.6 copy.15

commit v6 on v5

--- a/solution.py
+++ b/solution.py
@@ -35,7 +35,7 @@
     send_ref, near_ref, self_ref, scale_vmem, own_hbm, edge_hbm, cache_hbm, wself_hbm, wneigh_hbm, cot_hbm,
     out_ref, grad_ref,
     own, edge, wneigh, cache, cot, base, look, acc, both_t, delta,
-    pool, recv, xfer, got0, got1, sum1, got2, scale_ref,
+    extra, pool, recv, xfer, got0, got1, sum1, got2, scale_ref,
     load_sem, wself_sem, cache_sem, cot_sem,
     send_sem, recv_sem, swap_out, swap_in, pass_sem, take_sem, cross_out, cross_in, hop_out, hop_in, last_out, last_in,
 ):
@@ -77,6 +77,9 @@
         pl.semaphore_signal(barrier, inc=1, device_id=to, device_id_type=MESH)
 
     pl.semaphore_signal(barrier, inc=1, device_id=other, device_id_type=MESH)
+    for k in range(2):
+        source = dom_of(lax.rem(z + 1, 4), lax.rem(y + 4 - lax.rem(x + 3 + k, 4), 4), 1 - c)
+        pl.semaphore_signal(barrier, inc=1, device_id=(source, x), device_id_type=MESH)
 
     def offset(i):
         group, dz = lax.rem(x + lax.rem(i, 2), 4), i // 2
@@ -158,9 +161,32 @@
         both = recv.at[f, pl.ds(slot_of(lax.rem(x + 3 - lax.rem(i, 2), 4), i // 2, 0), 2)]
         return pltpu.make_async_copy(both, both, take_sem.at[f, i])
 
+    def forward(f, i, dc):
+        @pl.when((f < PHASES - 1) | (i < 6))
+        def _():
+            onward(f, i, dc).start()
+
+    def straight(k, dc):
+        group = lax.rem(x + 2 + k, 4)
+        to = dom_of(lax.rem(z + 3, 4), lax.rem(y + lax.rem(group + 1, 4), 4), c if dc == 0 else 1 - c)
+        return to, pltpu.make_async_remote_copy(
+            src_ref=extra.at[k, dc], dst_ref=recv.at[PHASES - 1, slot_of(group, 3, dc)],
+            send_sem=pass_sem, recv_sem=take_sem.at[PHASES - 1, 7 - k],
+            device_id=(to, x), device_id_type=MESH,
+        )
+
+    def send_straight():
+        for k in range(2):
+            for dc in range(2):
+                to, copy = straight(k, dc)
+                chosen = send_ref[0, to]
+                rows = own[chosen, :, (PHASES - 1) * WIDE:].astype(F32) * (scale_ref[chosen] * MOMENTUM)
+                extra[k, dc] = rows.astype(BF16).reshape(PIECE)
+                copy.start()
+
     def after_swap(f, i):
         swap(f, i).wait_recv()
-        onward(f, i, 1).start()
+        forward(f, i, 1)
         group, dz, _ = offset(i)
         combine(f, group, dz, 1)
 
@@ -212,7 +238,7 @@
 
     loads[0].wait()
     fill(0)
-    pl.semaphore_wait(barrier, 28)
+    pl.semaphore_wait(barrier, 30)
     for f in range(PHASES):
         if f:
             fill(f)
@@ -225,6 +251,7 @@
             for n in range(2):
                 cache_copy(n).start()
 
+    send_straight()
     for n in range(PHASES):
         wself_copy(n).start()
     for load in loads[1:]:
@@ -265,7 +292,7 @@
         @pl.loop(0, PAIRS)
         def _(i):
             arrive(f, i, 0)
-            onward(f, i, 0).start()
+            forward(f, i, 0)
 
             @pl.when(i < SWAP_LAG)
             def _():
@@ -440,6 +467,7 @@
             pltpu.VMEM((TARGETS, BLOCK, FEATS), F32),
             pltpu.VMEM((8 + TARGETS, FEATS, BLOCK), BF16),
             pltpu.VMEM((2, TARGETS, BLOCK, WIDE), BF16),
+            pltpu.VMEM((2, 2) + PIECE, BF16),
             pltpu.VMEM((PHASES, 2, 4, 4, 4, 16, WIDE), BF16),
             pltpu.VMEM((PHASES, 32) + PIECE, BF16),
             pltpu.VMEM((PHASES, 4, 4, 4, 16, WIDE), BF16),

time: 102 us -> 104 us (1.020)
  Pallas kernels: 98.2 us -> 100 us
    pallas_call x1, Pallas kernels: 98.2 us -> 100 us  [layer(): pl.pallas_call(functools.partial(layer_kernel, factor), out_shape=(pltpu....]
where the time goes in v6:
time: 104 us; the launch traced here: 103 us
  Pallas kernels  100 us (96%)
  local copies, waits for them, and re-layouts  2.64 us (3%)
    pallas_call x1, Pallas kernels, layer(): pl.pallas_call(functools.partial(layer_kernel, factor), out_shape=(pltpu....  100 us
    unnamed x2, local copies, waits for them, and re-layouts  2.64 us

profile of v6, /device:TPU:0, one launch (start us, length us, event | category | flops | bytes accessed | tf_op | source)
XLA Modules:
  0.0 103.4 jit_solution(10513477637431108586)
XLA Ops:
  0.6 100.1 %layer.1 = (bf16[16,128,1024]{2,1,0:T(8,128)(2,1)S(1)}, f32[16,1024]{1,0:T(8,128)S(1)}) custom-call(s32[1,32]{1,0:T(1,128)} %send_ref.1, s32[6,1,16]{2,1,0:T(1,128)} %bitcast.14, s32[1,16]{1,0:T(1,128)} %self_ref.1, bf16[1,8]{1,0:T(2,128)(2,1)} %bitcast.15, bf16[8,128,1024]{2,1,0:T(8,128)(2,1)} %bitcast.12, bf16[16,6,128,128]{3,2,1,0:T(8,128)(2,1)} %bitcast.11, ...), custom_call_target="tpu_custom_call" | custom-call | tf_op jit(solution)/shard_map/layer/pallas_call | solution.py:451
  100.8 2.0 %copy.14 = bf16[2048,1024]{1,0:T(8,128)(2,1)} copy(bf16[2048,1024]{1,0:T(8,128)(2,1)S(1)} %bitcast.8) | data formatting | bytes 8388608
  102.8 0.6 copy.15
